TPU v7x, 512 devices: a whole 4x8x8 slice. The times are simulated.
512 devices in a mesh: tm: 128 (over z, y, core), swath: 4 (over x).
Axes of the slice: x: 4, y: 8, z: 8, core: 2. Of those that a mesh axis runs over, the one named last changes fastest.
Arguments:
- design: bfloat16 [128, 2048, 512], P('tm', 'swath'), may hold values from -6 to 6
- process: bfloat16 [128, 512, 512], P('tm', 'swath')
- prior_prec: float32 [128, 512], P('tm', 'swath'), may hold values from 0.05 to 0.5
- routes: int32 [128, 16], P('tm', 'swath'), may hold values from -1 to 127, as said below
- counts: int32 [128, 4], P('tm', 'swath'), may hold values from 1 to 4
Outputs:
- reduced_diag: float32 [128, 512, 512], P('tm', 'swath')
- reduced_coupling: float32 [128, 512, 512], P('tm', 'swath')
Inputs may be any that keep to these rules, and one draw needn't show every extreme that they name: `routes`: each value is the holder's own time block i or i + 1, or -1 only where i + 1 would be 128; of one holder's 4 blocks, exactly 2 name i and the others i + 1 or -1.
All inputs are finite; a program needn't handle non-finite values.
Results may differ from a plain program's by a relative error of at most 0.00073.
Values may be sent and summed in bfloat16 or wider, within the bound.
No kernel may reach another device: no remote copies, remote signals or barrier semaphores. Data moves between devices by JAX's collectives and lax.ppermute only.
A program may use at most 64 MiB of HBM per device.

v0:
```python
import functools
import jax
import jax.numpy as jnp
from jax import lax
from jax.experimental import pallas as pl
from jax.experimental.pallas import tpu as pltpu
from jax.sharding import PartitionSpec as P

LEVELS = 3
NB = 128
WIDTH = 16
HALF = NB // 2
f32, bf16 = jnp.float32, jnp.bfloat16
VMEM = pl.BlockSpec(memory_space=pltpu.VMEM)
SMEM = pl.BlockSpec(memory_space=pltpu.SMEM)
PARAMS = pltpu.CompilerParams(vmem_limit_bytes=48 * 2**20)
KK, KM, MK = ((0,), (0,)), ((1,), (0,)), ((1,), (1,))


def mm(a, b, dims=KM):
    return lax.dot_general(a, b, (dims, ((), ())), preferred_element_type=f32)


def halves(x):
    high = x.astype(bf16)
    return high, (x - high.astype(f32)).astype(bf16)


def thirds(x):
    high = x.astype(bf16).astype(f32)
    rest = x - high
    mid = rest.astype(bf16).astype(f32)
    return high, mid, rest - mid


def split_dot(a, b, dims=KM):
    return mm(a[0], b[0], dims) + (mm(a[0], b[1], dims) + mm(a[1], b[0], dims))


def block_inverse(a):
    lane = lax.broadcasted_iota(jnp.int32, (WIDTH, NB), 1)
    row = lax.broadcasted_iota(jnp.int32, (WIDTH, NB), 0)
    lane_all = lax.broadcasted_iota(jnp.int32, (NB, NB), 1)
    p = a[:WIDTH, :]
    for start in range(0, NB, WIDTH):
        stop = start + WIDTH
        inside = (lane >= start) & (lane < stop)
        cols = [jnp.broadcast_to(p[:, start + j : start + j + 1], (WIDTH, NB)) for j in range(WIDTH)]
        h, m, l = thirds(jnp.where(inside, 0.0, jnp.where(lane < start, -p, p)))
        lhs = jnp.concatenate([h, h, m, h, l, m], axis=0).T.astype(bf16)
        x = jnp.where(inside, jnp.where(lane - start == row, 1.0, 0.0), p)
        if stop < NB:
            after = a[stop : stop + WIDTH, :]
            weights = [jnp.broadcast_to(after[:, start + j : start + j + 1], (WIDTH, NB)) for j in range(WIDTH)]
        for j in range(WIDTH):
            c = cols[j]
            scale = 1.0 / c[j : j + 1, :]
            here = row == j

            def step(v):
                t = v[j : j + 1, :] * scale
                return jnp.where(here, t, v - c * t)

            for i in range(j + 1, WIDTH):
                cols[i] = step(cols[i])
            x = step(x)
        if stop < NB:
            sums = [weights[j] * x[j : j + 1, :] for j in range(4)]
            for j in range(4, WIDTH):
                sums[j % 4] = sums[j % 4] + weights[j] * x[j : j + 1, :]
            p = jnp.where(inside, 0.0, after) - ((sums[0] + sums[1]) + (sums[2] + sums[3]))
        h, m, l = thirds(x)
        rhs = jnp.concatenate([h, m, h, l, h, m], axis=0).astype(bf16)
        a = jnp.where((lane_all >= start) & (lane_all < stop), 0.0, a) - mm(lhs, rhs)
        rows = [x]
        if start:
            rows = [a[:start]] + rows
        if stop < NB:
            rows = rows + [a[stop:]]
        a = jnp.concatenate(rows, axis=0)
    return a


def inverse_kernel(with_rows, sid_ref, g_ref, x_ref, *rest):
    size = x_ref.shape[0]
    count = size // NB
    for k in range(count):
        s, n = slice(k * NB, (k + 1) * NB), (k + 1) % count
        t = slice(n * NB, (n + 1) * NB)
        x_ref[s, s] = g_ref[k, :NB, :]
        block = g_ref[k, NB : 2 * NB, :]
        x_ref[s, t] = block
        x_ref[t, s] = block.T
    for p in range(2):
        s, t = slice(p * NB, (p + 1) * NB), slice((p + 2) * NB, (p + 3) * NB)
        block = jnp.concatenate([g_ref[p, 2 * NB :, :], g_ref[p + 2, 2 * NB :, :]], axis=0)
        x_ref[s, t] = block
        x_ref[t, s] = block.T
    if with_rows:
        rest[0][...] = x_ref[pl.ds(pl.multiple_of(sid_ref[0] * NB, NB), NB), :]
    left_t = rest[-1]
    lane = lax.broadcasted_iota(jnp.int32, (NB, size), 1)

    def eliminate(b, carry):
        first = pl.multiple_of(b * NB, NB)
        at = pl.ds(first, NB)
        inv = block_inverse(x_ref[at, at])
        rows = x_ref[at, :]
        inside = (lane >= first) & (lane < first + NB)
        left_t[...] = jnp.where(lane < first, -rows, rows).T
        w = split_dot(halves(inv), halves(jnp.where(inside, 0.0, rows)))
        w = jnp.where(inside, jnp.concatenate([inv] * count, axis=1), w)
        w_halves = halves(w)
        for i in range(1, count):
            other = pl.ds(pl.multiple_of(lax.rem(b + i, count) * NB, NB), NB)
            x_ref[other, :] = jnp.where(inside, 0.0, x_ref[other, :]) - split_dot(halves(left_t[other, :]), w_halves)
        x_ref[at, :] = w
        return carry

    lax.fori_loop(0, count, eliminate, 0)


def inverse(sid, g, with_rows=False):
    size = 4 * NB
    outs = [jax.ShapeDtypeStruct((size, size), f32)]
    if with_rows:
        outs.append(jax.ShapeDtypeStruct((NB, size), f32))
    return pl.pallas_call(
        functools.partial(inverse_kernel, with_rows),
        out_shape=outs,
        in_specs=[SMEM, VMEM],
        out_specs=[VMEM] * len(outs),
        scratch_shapes=[pltpu.VMEM((size, NB), f32)],
        compiler_params=PARAMS,
        cost_estimate=pl.CostEstimate(flops=60 * size**3, bytes_accessed=8 * size * size, transcendentals=0),
        name="inverse",
    )(sid, g)


def weigh_kernel(total_slots, ids_ref, design_ref, process_ref, own_ref, ahead_ref):
    rows = own_ref.shape[0] // 2
    me, live_count = ids_ref[0], ids_ref[1]
    own_seen = jnp.int32(0)
    for r in range(4):
        target = ids_ref[2 + r]
        is_own = target == me
        live = (r < live_count) & (is_own | (target == me + 1))
        h = design_ref[r * rows : (r + 1) * rows, :].astype(f32)
        mean_sq = jnp.mean(h * h, axis=-1, keepdims=True)
        w = h * lax.rsqrt(4.0 * total_slots * (mean_sq + 1e-06))
        w = jnp.where(live, w, 0.0).astype(bf16)
        ahead_seen = r - own_seen

        @pl.when(is_own)
        def _():
            own_ref[pl.ds(jnp.minimum(own_seen, 1) * rows, rows), :] = w

        @pl.when(jnp.logical_not(is_own))
        def _():
            ahead_ref[pl.ds(jnp.minimum(ahead_seen, 1) * rows, rows), :] = w

        own_seen = own_seen + jnp.where(is_own, 1, 0)
    ahead_ref[2 * rows :, :] = process_ref[...]


def gram_kernel(own_ref, incoming_ref, out_ref):
    both = jnp.concatenate([own_ref[...], incoming_ref[: own_ref.shape[0], :]], axis=0)
    g = mm(both, both, KK)
    for k in range(4):
        n, p, h = (k + 1) % 4, k % 2, HALF * (k // 2)
        out_ref[k, :NB, :] = g[k * NB : (k + 1) * NB, k * NB : (k + 1) * NB]
        out_ref[k, NB : 2 * NB, :] = g[k * NB : (k + 1) * NB, n * NB : (n + 1) * NB]
        out_ref[k, 2 * NB :, :] = g[p * NB + h : p * NB + h + HALF, (p + 2) * NB : (p + 3) * NB]


def start_kernel(sid_ref, parts_ref, own_ref, incoming_ref, prior_ref, d_ref, copies_ref):
    q = sid_ref[0]
    rows = own_ref[...].astype(f32) + incoming_ref[incoming_ref.shape[0] - NB :, :].astype(f32)
    total = (parts_ref[0] + parts_ref[1]) + (parts_ref[2] + parts_ref[3])

    def block(k):
        out = rows[:, :NB]
        for j in range(1, 4):
            out = jnp.where(k == j, rows[:, j * NB : (j + 1) * NB], out)
        return out

    unit = lax.broadcasted_iota(jnp.int32, (NB, NB), 0) == lax.broadcasted_iota(jnp.int32, (NB, NB), 1)
    across = block(lax.rem(q + 2, 4))
    half = jnp.where(q < 2, across[:HALF, :], across.T[HALF:, :])
    d = jnp.concatenate(
        [
            total[:NB] + (block(q) + jnp.where(unit, prior_ref[...], 0.0)),
            total[NB : 2 * NB] + block(lax.rem(q + 1, 4)),
            total[2 * NB :] + half,
        ],
        axis=0,
    )
    d_ref[...] = d
    for k in range(4):
        copies_ref[k] = d


def next_kernel(d_in, left_ref, right_ref, d_ref, copies_ref):
    d = d_in[...] - left_ref[...] - right_ref[...]
    d_ref[...] = d
    for k in range(4):
        copies_ref[k] = d


def sliced_terms_kernel(sid_ref, x_ref, a_ref, c_ref, right_term, left_term, lhs, flipped):
    q = sid_ref[0]
    p, h = lax.rem(q, 2), pl.multiple_of(lax.div(q, 2) * HALF, HALF)

    def at(k):
        return pl.ds(pl.multiple_of(k * NB, NB), NB)

    own, after, across = at(q), at(lax.rem(q + 1, 4)), at(p + 2)
    lhs[:NB, :] = a_ref[own, :].astype(f32)
    lhs[NB : NB + HALF, :] = a_ref[pl.ds(pl.multiple_of(p * NB + h, HALF), HALF), :].astype(f32)
    lhs[NB + HALF : 2 * NB + HALF, :] = c_ref[:, own].astype(f32).T
    flipped[...] = c_ref[:, at(p)].astype(f32).T
    lhs[2 * NB + HALF :, :] = flipped[pl.ds(h, HALF), :]
    z = halves(split_dot(halves(lhs[...]), halves(x_ref[...])))

    def rows(first, count):
        return z[0][first : first + count], z[1][first : first + count]

    full, part = rows(0, NB), rows(NB, HALF)
    right_term[:NB, :] = cross_dot(full, a_ref[own, :], MK)
    right_term[NB : 2 * NB, :] = cross_dot(full, a_ref[after, :], MK)
    right_term[2 * NB :, :] = cross_dot(part, a_ref[across, :], MK)
    full, part = rows(NB + HALF, NB), rows(2 * NB + HALF, HALF)
    left_term[:NB, :] = cross_dot(full, c_ref[:, own])
    left_term[NB : 2 * NB, :] = cross_dot(full, c_ref[:, after])
    left_term[2 * NB :, :] = cross_dot(part, c_ref[:, across])


def sliced_terms(sid, x, a, c):
    size = x.shape[0]
    out = jax.ShapeDtypeStruct((2 * NB + HALF, NB), f32)
    return pl.pallas_call(
        sliced_terms_kernel,
        out_shape=(out, out),
        in_specs=[SMEM] + [VMEM] * 3,
        out_specs=(VMEM, VMEM),
        scratch_shapes=[pltpu.VMEM((3 * NB, size), f32), pltpu.VMEM((NB, size), f32)],
        compiler_params=PARAMS,
        cost_estimate=pl.CostEstimate(flops=4 * size**3, bytes_accessed=16 * size * size, transcendentals=0),
        name="sliced_terms",
    )(sid, x, a, c)


def terms_kernel(sid_ref, x_ref, a_ref, c_ref, *outs):
    col = pl.multiple_of(sid_ref[0] * NB, NB)
    lhs = jnp.concatenate([a_ref[pl.ds(col, NB), :].astype(f32), c_ref[:, pl.ds(col, NB)].astype(f32).T], axis=0)
    z = halves(split_dot(halves(lhs), halves(x_ref[...])))
    top = z[0][:NB], z[1][:NB]
    outs[0][...] = cross_dot(top, a_ref[...], MK).astype(bf16)
    both = cross_dot(z, c_ref[...])
    outs[1][...] = both[NB:].astype(bf16)
    outs[2][...] = -both[:NB]


def cross_dot(a, b, dims=KM):
    if b.dtype == bf16:
        return mm(a[0], b, dims) + mm(a[1], b, dims)
    return split_dot(a, halves(b), dims)


def terms(sid, x, a, c):
    size = x.shape[0]
    term = jax.ShapeDtypeStruct((NB, size), bf16)
    return pl.pallas_call(
        terms_kernel,
        out_shape=(term, term, jax.ShapeDtypeStruct((NB, size), f32)),
        in_specs=[SMEM] + [VMEM] * 3,
        out_specs=(VMEM,) * 3,
        compiler_params=PARAMS,
        cost_estimate=pl.CostEstimate(flops=4 * size**3, bytes_accessed=16 * size * size, transcendentals=0),
        name="terms",
    )(sid, x, a, c)


def coupling_kernel(x_ref, a_ref, c_ref, n_ref):
    x = halves(x_ref[...])
    if a_ref.dtype == bf16:
        z = mm(a_ref[...], x[0]) + mm(a_ref[...], x[1])
    else:
        z = split_dot(halves(a_ref[...]), x)
    n_ref[...] = -cross_dot(halves(z), c_ref[...])


def coupled(x, a, c):
    size = x.shape[0]
    return pl.pallas_call(
        coupling_kernel,
        out_shape=jax.ShapeDtypeStruct(x.shape, f32),
        in_specs=[VMEM] * 3,
        out_specs=VMEM,
        compiler_params=PARAMS,
        cost_estimate=pl.CostEstimate(flops=12 * size**3, bytes_accessed=16 * size * size, transcendentals=0),
        name="coupling",
    )(x, a, c)


def passed_along(block, axis, distance, around=False):
    count = lax.axis_size(axis)
    route = [(i, (i + distance) % count) for i in range(count) if around or 0 <= i + distance < count]
    return lax.ppermute(block, axis, route)


def exchanged(blocks):
    return lax.all_to_all(blocks, "swath", 0, 0, tiled=True)


def shards(design, process, prior_prec, routes, counts):
    row_count, size = process.shape[1:]
    swaths = lax.axis_size("swath")
    me = lax.axis_index("tm")
    sid = lax.axis_index("swath")
    total_slots = design.shape[1] * swaths
    ids = jnp.concatenate([me[None].astype(jnp.int32), counts[0], routes[0]])
    sids = sid[None].astype(jnp.int32)
    half = design.shape[1] // 2
    own, ahead = pl.pallas_call(
        functools.partial(weigh_kernel, total_slots),
        out_shape=(
            jax.ShapeDtypeStruct((half, size), bf16),
            jax.ShapeDtypeStruct((half + row_count, size), bf16),
        ),
        in_specs=[SMEM] + [VMEM] * 2,
        out_specs=(VMEM, VMEM),
        compiler_params=PARAMS,
        name="weigh",
    )(ids, design[0], process[0])
    incoming = passed_along(ahead, "tm", 1)
    cut = jax.ShapeDtypeStruct((2 * NB + HALF, NB), f32)
    cuts = jax.ShapeDtypeStruct((swaths,) + cut.shape, f32)
    parts = pl.pallas_call(
        gram_kernel,
        out_shape=cuts,
        in_specs=[VMEM] * 2,
        out_specs=VMEM,
        compiler_params=PARAMS,
        name="gram",
    )(own, incoming)
    diag, copies = pl.pallas_call(
        start_kernel,
        out_shape=(cut, cuts),
        in_specs=[SMEM] + [VMEM] * 4,
        out_specs=(VMEM, VMEM),
        compiler_params=PARAMS,
        name="start",
    )(sids, exchanged(parts), process[0], incoming, prior_prec)
    pair = jnp.concatenate([incoming[half:], process[0]], axis=0)
    pairs = jnp.broadcast_to(pair[None], (swaths,) + pair.shape)
    copies, pairs = lax.optimization_barrier((copies, pairs))
    all_diag = exchanged(copies)
    pairs = exchanged(pairs)
    (x,) = inverse(sids, all_diag)
    a = pairs[:, :row_count].reshape(size, size)
    c = pairs[:, row_count:].reshape(size, size)
    rows = None
    for level in range(LEVELS):
        distance = 2**level
        if level == LEVELS - 1:
            out = terms(sids, x, a, c)
            from_right = passed_along(out[0], "tm", -distance)
            from_left = passed_along(out[1], "tm", distance)
            coupling = passed_along(out[2], "tm", -distance)
            return ((rows - from_left.astype(f32) - from_right.astype(f32))[None], coupling[None])
        right_term, left_term = sliced_terms(sids, x, a, c)
        from_right = passed_along(right_term, "tm", -distance)
        from_left = passed_along(left_term, "tm", distance)
        n = coupled(x, a, c)
        from_right, from_left, n = lax.optimization_barrier((from_right, from_left, n))
        diag, copies = pl.pallas_call(
            next_kernel,
            out_shape=(cut, cuts),
            in_specs=[VMEM] * 3,
            out_specs=(VMEM, VMEM),
            compiler_params=PARAMS,
            name="next",
        )(diag, from_left, from_right)
        x, *tail = inverse(sids, exchanged(copies), level == LEVELS - 2)
        rows = tail[0] if tail else None
        a = passed_along(n, "tm", distance)
        c = passed_along(n, "tm", -distance)


def solution(mesh):
    return jax.shard_map(
        shards,
        mesh=mesh,
        in_specs=(
            P("tm", "swath", None),
            P("tm", "swath", None),
            P("tm", "swath"),
            P("tm", "swath"),
            P("tm", "swath"),
        ),
        out_specs=(P("tm", "swath", None), P("tm", "swath", None)),
        check_vma=False,
    )
```

profile of v0, /device:TPU:242, one launch (start us, length us, event | category | flops | bytes accessed | tf_op | source)
XLA Modules:
  0.0 192.6 jit_solution(7698799524220688143)
XLA Ops:
  1.3 0.6 copy-done.4
  1.9 0.1 pad_add_fusion.ids_ref
  2.0 0.9 copy-done
  2.9 1.0 copy-done.2
  4.0 1.1 weigh.1
  5.0 1.9 collective-permute-start
  7.0 7.2 %collective-permute-done.incoming_ref = bf16[384,512]{1,0:T(8,128)(2,1)S(1)} collective-permute-done((bf16[384,512]{1,0:T(8,128)(2,1)S(1)}, bf16[384,512]{1,0:T(8,128)(2,1)S(1)}, u32[]{:S(2)}, u32[]{:S(2)}) %collective-permute-start) | collective-permute-done | bytes 393248 | tf_op jit(solution)/shard_map/ppermute | solution.py:309
  14.1 1.3 gram.1
  15.4 4.8 %all-to-all-start = ((f32[4,320,128]{2,1,0:T(8,128)}), f32[4,320,128]{2,1,0:T(8,128)S(1)}, u32[]{:S(2)}, u32[]{:S(2)}) async-start(f32[4,320,128]{2,1,0:T(8,128)} %gram.1), calls=%async_computation | async-start | bytes 1310720 | tf_op jit(solution)/shard_map/all_to_all | solution.py:313
  20.3 0.9 copy-done.1
  21.2 7.0 %all-to-all-done.parts_ref = f32[4,320,128]{2,1,0:T(8,128)S(1)} async-done(((f32[4,320,128]{2,1,0:T(8,128)}), f32[4,320,128]{2,1,0:T(8,128)S(1)}, u32[]{:S(2)}, u32[]{:S(2)}) %all-to-all-start) | async-done | bytes 655392 | tf_op jit(solution)/shard_map/all_to_all | solution.py:313
  28.2 0.1 start.1
  28.3 1.1 broadcast_in_dim.20
  29.4 11.2 %all_to_all.25.g_ref = f32[4,320,128]{2,1,0:T(8,128)S(1)} all-to-all(f32[4,320,128]{2,1,0:T(8,128)S(1)} %get-tuple-element.30), channel_id=1, replica_groups=mesh['tm'=128,'swath'=4] {'swath'}, dimensions={0} | all-to-all | bytes 1310720 | tf_op jit(solution)/shard_map/all_to_all | solution.py:313
  40.6 4.9 %all-to-all-start.2 = ((bf16[4,256,512]{2,1,0:T(8,128)(2,1)}), bf16[4,256,512]{2,1,0:T(8,128)(2,1)S(1)}, u32[]{:S(2)}, u32[]{:S(2)}) async-start(bf16[4,256,512]{2,1,0:T(8,128)(2,1)} %broadcast_in_dim.20), calls=%async_computation.2 | async-start | bytes 2097152 | tf_op jit(solution)/shard_map/all_to_all | solution.py:313
  45.5 14.0 %inverse.3.x_ref = f32[512,512]{1,0:T(8,128)S(1)} custom-call(s32[1]{0:T(128)} %bitcast.sid_ref, f32[4,320,128]{2,1,0:T(8,128)S(1)} %all_to_all.25.g_ref), custom_call_target="tpu_custom_call" | custom-call | flops 8053063680 | bytes 2097152 | tf_op jit(solution)/shard_map/inverse/pallas_call | solution.py:128
  59.5 0.1 fusion
  59.6 1.3 sliced_terms.2
  60.9 1.9 collective-permute-start.1
  62.9 2.4 %collective-permute-start.2 = (f32[320,128]{1,0:T(8,128)S(1)}, f32[320,128]{1,0:T(8,128)S(1)}, u32[]{:S(2)}, u32[]{:S(2)}) collective-permute-start(f32[320,128]{1,0:T(8,128)S(1)} %get-tuple-element.33), channel_id=1, source_target_pairs={{0,4},{4,8},{8,12},{12,16},{16,20},{20,24},{24,28},{28,32},{32,36}... | collective-permute-start | bytes 491528 | tf_op jit(solution)/shard_map/ppermute | solution.py:309
  65.3 2.3 %coupling.2 = f32[512,512]{1,0:T(8,128)} custom-call(f32[512,512]{1,0:T(8,128)S(1)} %inverse.3.x_ref, bf16[512,512]{1,0:T(8,128)(2,1)S(1)} %bitcast.15, bf16[512,512]{1,0:T(8,128)(2,1)S(1)} %bitcast.13), custom_call_target="tpu_custom_call" | custom-call | flops 1610612736 | bytes 4194304 | tf_op jit(solution)/shard_map/coupling/pallas_call | solution.py:295
  67.5 2.0 %collective-permute-done.2.left_ref = f32[320,128]{1,0:T(8,128)S(1)} collective-permute-done((f32[320,128]{1,0:T(8,128)S(1)}, f32[320,128]{1,0:T(8,128)S(1)}, u32[]{:S(2)}, u32[]{:S(2)}) %collective-permute-start.2) | collective-permute-done | bytes 163872 | tf_op jit(solution)/shard_map/ppermute | solution.py:309
  69.5 0.9 next.2
  70.4 4.8 %all-to-all-start.3 = ((f32[4,320,128]{2,1,0:T(8,128)}), f32[4,320,128]{2,1,0:T(8,128)S(1)}, u32[]{:S(2)}, u32[]{:S(2)}) async-start(f32[4,320,128]{2,1,0:T(8,128)} %get-tuple-element.37), calls=%async_computation.3 | async-start | bytes 1310720 | tf_op jit(solution)/shard_map/all_to_all | solution.py:313
  75.2 3.7 %collective-permute-start.3 = (f32[512,512]{1,0:T(8,128)}, f32[512,512]{1,0:T(8,128)S(1)}, u32[]{:S(2)}, u32[]{:S(2)}) collective-permute-start(f32[512,512]{1,0:T(8,128)} %coupling.2), channel_id=1, source_target_pairs={{0,4},{4,8},{8,12},{12,16},{16,20},{20,24},{24,28},{28,32},{32,36}... | collective-permute-start | bytes 3145736 | tf_op jit(solution)/shard_map/ppermute | solution.py:309
  78.9 1.9 collective-permute-start.4
  80.8 4.1 %all-to-all-done.3.g_ref = f32[4,320,128]{2,1,0:T(8,128)S(1)} async-done(((f32[4,320,128]{2,1,0:T(8,128)}), f32[4,320,128]{2,1,0:T(8,128)S(1)}, u32[]{:S(2)}, u32[]{:S(2)}) %all-to-all-start.3) | async-done | bytes 655392 | tf_op jit(solution)/shard_map/all_to_all | solution.py:313
  85.0 14.0 %inverse.4.x_ref = f32[512,512]{1,0:T(8,128)S(1)} custom-call(s32[1]{0:T(128)} %bitcast.sid_ref, f32[4,320,128]{2,1,0:T(8,128)S(1)} %all-to-all-done.3.g_ref), custom_call_target="tpu_custom_call" | custom-call | flops 8053063680 | bytes 2097152 | tf_op jit(solution)/shard_map/inverse/pallas_call | solution.py:128
  99.0 1.6 sliced_terms.3
  100.6 1.9 collective-permute-start.5
  102.5 7.3 %collective-permute-start.6 = (f32[320,128]{1,0:T(8,128)S(1)}, f32[320,128]{1,0:T(8,128)S(1)}, u32[]{:S(2)}, u32[]{:S(2)}) collective-permute-start(f32[320,128]{1,0:T(8,128)S(1)} %get-tuple-element.40), channel_id=1, source_target_pairs={{0,8},{4,12},{8,16},{12,20},{16,24},{20,28},{24,32},{28,36},{32,40... | collective-permute-start | bytes 491528 | tf_op jit(solution)/shard_map/ppermute | solution.py:309
  109.8 2.8 %coupling.3 = f32[512,512]{1,0:T(8,128)} custom-call(f32[512,512]{1,0:T(8,128)S(1)} %inverse.4.x_ref, f32[512,512]{1,0:T(8,128)S(1)} %collective-permute-done.3.a_ref, f32[512,512]{1,0:T(8,128)S(1)} %collective-permute-done.4.c_ref), custom_call_target="tpu_custom_call" | custom-call | flops 1610612736 | bytes 4194304 | tf_op jit(solution)/shard_map/coupling/pallas_call | solution.py:295
  112.6 0.9 next.3
  113.6 5.2 %all-to-all-start.4 = ((f32[4,320,128]{2,1,0:T(8,128)}), f32[4,320,128]{2,1,0:T(8,128)S(1)}, u32[]{:S(2)}, u32[]{:S(2)}) async-start(f32[4,320,128]{2,1,0:T(8,128)} %get-tuple-element.43), calls=%async_computation.4 | async-start | bytes 1310720 | tf_op jit(solution)/shard_map/all_to_all | solution.py:313
  118.8 7.5 %collective-permute-start.7 = (f32[512,512]{1,0:T(8,128)}, f32[512,512]{1,0:T(8,128)S(1)}, u32[]{:S(2)}, u32[]{:S(2)}) collective-permute-start(f32[512,512]{1,0:T(8,128)} %coupling.3), channel_id=1, source_target_pairs={{0,8},{4,12},{8,16},{12,20},{16,24},{20,28},{24,32},{28,36},{32,40... | collective-permute-start | bytes 3145736 | tf_op jit(solution)/shard_map/ppermute | solution.py:309
  126.3 1.9 collective-permute-start.8
  128.3 14.0 %inverse.5 = (f32[512,512]{1,0:T(8,128)S(1)}, f32[128,512]{1,0:T(8,128)S(1)}) custom-call(s32[1]{0:T(128)} %bitcast.sid_ref, f32[4,320,128]{2,1,0:T(8,128)S(1)} %all-to-all-done.4.g_ref), custom_call_target="tpu_custom_call" | custom-call | flops 8053063680 | bytes 2097152 | tf_op jit(solution)/shard_map/inverse/pallas_call | solution.py:128
  142.3 7.0 %collective-permute-done.7.a_ref = f32[512,512]{1,0:T(8,128)S(1)} collective-permute-done((f32[512,512]{1,0:T(8,128)}, f32[512,512]{1,0:T(8,128)S(1)}, u32[]{:S(2)}, u32[]{:S(2)}) %collective-permute-start.7) | collective-permute-done | bytes 1048608 | tf_op jit(solution)/shard_map/ppermute | solution.py:309
  149.3 11.6 %collective-permute-done.8.c_ref = f32[512,512]{1,0:T(8,128)S(1)} collective-permute-done((f32[512,512]{1,0:T(8,128)}, f32[512,512]{1,0:T(8,128)S(1)}, u32[]{:S(2)}, u32[]{:S(2)}) %collective-permute-start.8) | collective-permute-done | bytes 1048608 | tf_op jit(solution)/shard_map/ppermute | solution.py:309
  160.9 1.6 terms.1
  162.5 1.9 collective-permute-start.10
  164.4 8.1 %collective-permute-start.9 = (bf16[128,512]{1,0:T(8,128)(2,1)S(1)}, bf16[128,512]{1,0:T(8,128)(2,1)S(1)}, u32[]{:S(2)}, u32[]{:S(2)}) collective-permute-start(bf16[128,512]{1,0:T(8,128)(2,1)S(1)} %get-tuple-element.47), channel_id=1, source_target_pairs={{0,16},{4,20},{8,24},{12,28},{16,32},{20,36},{24,40},{28,44},{32,4... | collective-permute-start | bytes 393224 | tf_op jit(solution)/shard_map/ppermute | solution.py:309
  172.6 1.9 collective-permute-start.11
  174.5 2.3 %collective-permute-done.10 = bf16[128,512]{1,0:T(8,128)(2,1)S(1)} collective-permute-done((bf16[128,512]{1,0:T(8,128)(2,1)S(1)}, bf16[128,512]{1,0:T(8,128)(2,1)S(1)}, u32[]{:S(2)}, u32[]{:S(2)}) %collective-permute-start.10) | collective-permute-done | bytes 131104 | tf_op jit(solution)/shard_map/ppermute | solution.py:309
  176.8 0.4 collective-permute-done.9
  177.2 0.7 subtract_bitcast_fusion
  178.0 13.9 %collective-permute-done.11 = f32[128,512]{1,0:T(8,128)S(1)} collective-permute-done((f32[128,512]{1,0:T(8,128)S(1)}, f32[128,512]{1,0:T(8,128)S(1)}, u32[]{:S(2)}, u32[]{:S(2)}) %collective-permute-start.11) | collective-permute-done | bytes 262176 | tf_op jit(solution)/shard_map/ppermute | solution.py:309
  191.9 0.7 copy.9
  (15 shorter events, 0.1 us)
Async XLA Ops:
  1.3 0.7 copy-start.4
  2.0 0.9 copy-start
  2.9 1.0 copy-start.2
  5.0 9.1 %collective-permute-start = (bf16[384,512]{1,0:T(8,128)(2,1)S(1)}, bf16[384,512]{1,0:T(8,128)(2,1)S(1)}, u32[]{:S(2)}, u32[]{:S(2)}) collective-permute-start(bf16[384,512]{1,0:T(8,128)(2,1)S(1)} %get-tuple-element.27), channel_id=1, source_target_pairs={{0,4},{4,8},{8,12},{12,16},{16,20},{20,24},{24,28},{28,32},{32,36}... | collective-permute-start | bytes 1179656 | tf_op jit(solution)/shard_map/ppermute | solution.py:309
  15.4 12.7 %all-to-all-start = ((f32[4,320,128]{2,1,0:T(8,128)}), f32[4,320,128]{2,1,0:T(8,128)S(1)}, u32[]{:S(2)}, u32[]{:S(2)}) async-start(f32[4,320,128]{2,1,0:T(8,128)} %gram.1), calls=%async_computation | async-start | bytes 1310720 | tf_op jit(solution)/shard_map/all_to_all | solution.py:313
  20.3 0.9 copy-start.1
  21.2 7.0 %copy-start.3 = (f32[1,128]{1,0:T(1,128)S(1)}, f32[1,128]{1,0:T(1,128)}, u32[]{:S(2)}) copy-start(f32[1,128]{1,0:T(1,128)} %prior_ref.1) | copy-start | bytes 1540
  40.6 19.0 %all-to-all-start.2 = ((bf16[4,256,512]{2,1,0:T(8,128)(2,1)}), bf16[4,256,512]{2,1,0:T(8,128)(2,1)S(1)}, u32[]{:S(2)}, u32[]{:S(2)}) async-start(bf16[4,256,512]{2,1,0:T(8,128)(2,1)} %broadcast_in_dim.20), calls=%async_computation.2 | async-start | bytes 2097152 | tf_op jit(solution)/shard_map/all_to_all | solution.py:313
  60.9 6.6 %collective-permute-start.1 = (f32[320,128]{1,0:T(8,128)S(1)}, f32[320,128]{1,0:T(8,128)S(1)}, u32[]{:S(2)}, u32[]{:S(2)}) collective-permute-start(f32[320,128]{1,0:T(8,128)S(1)} %get-tuple-element.32), channel_id=1, source_target_pairs={{4,0},{8,4},{12,8},{16,12},{20,16},{24,20},{28,24},{32,28},{36,32}... | collective-permute-start | bytes 491528 | tf_op jit(solution)/shard_map/ppermute | solution.py:309
  62.9 6.6 %collective-permute-start.2 = (f32[320,128]{1,0:T(8,128)S(1)}, f32[320,128]{1,0:T(8,128)S(1)}, u32[]{:S(2)}, u32[]{:S(2)}) collective-permute-start(f32[320,128]{1,0:T(8,128)S(1)} %get-tuple-element.33), channel_id=1, source_target_pairs={{0,4},{4,8},{8,12},{12,16},{16,20},{20,24},{24,28},{28,32},{32,36}... | collective-permute-start | bytes 491528 | tf_op jit(solution)/shard_map/ppermute | solution.py:309
  70.4 14.6 %all-to-all-start.3 = ((f32[4,320,128]{2,1,0:T(8,128)}), f32[4,320,128]{2,1,0:T(8,128)S(1)}, u32[]{:S(2)}, u32[]{:S(2)}) async-start(f32[4,320,128]{2,1,0:T(8,128)} %get-tuple-element.37), calls=%async_computation.3 | async-start | bytes 1310720 | tf_op jit(solution)/shard_map/all_to_all | solution.py:313
  75.2 23.8 %collective-permute-start.3 = (f32[512,512]{1,0:T(8,128)}, f32[512,512]{1,0:T(8,128)S(1)}, u32[]{:S(2)}, u32[]{:S(2)}) collective-permute-start(f32[512,512]{1,0:T(8,128)} %coupling.2), channel_id=1, source_target_pairs={{0,4},{4,8},{8,12},{12,16},{16,20},{20,24},{24,28},{28,32},{32,36}... | collective-permute-start | bytes 3145736 | tf_op jit(solution)/shard_map/ppermute | solution.py:309
  78.9 20.1 %collective-permute-start.4 = (f32[512,512]{1,0:T(8,128)}, f32[512,512]{1,0:T(8,128)S(1)}, u32[]{:S(2)}, u32[]{:S(2)}) collective-permute-start(f32[512,512]{1,0:T(8,128)} %coupling.2), channel_id=1, source_target_pairs={{4,0},{8,4},{12,8},{16,12},{20,16},{24,20},{28,24},{32,28},{36,32}... | collective-permute-start | bytes 3145736 | tf_op jit(solution)/shard_map/ppermute | solution.py:309
  100.6 12.0 %collective-permute-start.5 = (f32[320,128]{1,0:T(8,128)S(1)}, f32[320,128]{1,0:T(8,128)S(1)}, u32[]{:S(2)}, u32[]{:S(2)}) collective-permute-start(f32[320,128]{1,0:T(8,128)S(1)} %get-tuple-element.39), channel_id=1, source_target_pairs={{8,0},{12,4},{16,8},{20,12},{24,16},{28,20},{32,24},{36,28},{40,32... | collective-permute-start | bytes 491528 | tf_op jit(solution)/shard_map/ppermute | solution.py:309
  102.5 10.1 %collective-permute-start.6 = (f32[320,128]{1,0:T(8,128)S(1)}, f32[320,128]{1,0:T(8,128)S(1)}, u32[]{:S(2)}, u32[]{:S(2)}) collective-permute-start(f32[320,128]{1,0:T(8,128)S(1)} %get-tuple-element.40), channel_id=1, source_target_pairs={{0,8},{4,12},{8,16},{12,20},{16,24},{20,28},{24,32},{28,36},{32,40... | collective-permute-start | bytes 491528 | tf_op jit(solution)/shard_map/ppermute | solution.py:309
  113.6 14.7 %all-to-all-start.4 = ((f32[4,320,128]{2,1,0:T(8,128)}), f32[4,320,128]{2,1,0:T(8,128)S(1)}, u32[]{:S(2)}, u32[]{:S(2)}) async-start(f32[4,320,128]{2,1,0:T(8,128)} %get-tuple-element.43), calls=%async_computation.4 | async-start | bytes 1310720 | tf_op jit(solution)/shard_map/all_to_all | solution.py:313
  118.8 30.6 %collective-permute-start.7 = (f32[512,512]{1,0:T(8,128)}, f32[512,512]{1,0:T(8,128)S(1)}, u32[]{:S(2)}, u32[]{:S(2)}) collective-permute-start(f32[512,512]{1,0:T(8,128)} %coupling.3), channel_id=1, source_target_pairs={{0,8},{4,12},{8,16},{12,20},{16,24},{20,28},{24,32},{28,36},{32,40... | collective-permute-start | bytes 3145736 | tf_op jit(solution)/shard_map/ppermute | solution.py:309
  126.3 34.6 %collective-permute-start.8 = (f32[512,512]{1,0:T(8,128)}, f32[512,512]{1,0:T(8,128)S(1)}, u32[]{:S(2)}, u32[]{:S(2)}) collective-permute-start(f32[512,512]{1,0:T(8,128)} %coupling.3), channel_id=1, source_target_pairs={{8,0},{12,4},{16,8},{20,12},{24,16},{28,20},{32,24},{36,28},{40,32... | collective-permute-start | bytes 3145736 | tf_op jit(solution)/shard_map/ppermute | solution.py:309
  162.5 14.3 %collective-permute-start.10 = (bf16[128,512]{1,0:T(8,128)(2,1)S(1)}, bf16[128,512]{1,0:T(8,128)(2,1)S(1)}, u32[]{:S(2)}, u32[]{:S(2)}) collective-permute-start(bf16[128,512]{1,0:T(8,128)(2,1)S(1)} %get-tuple-element.48), channel_id=1, source_target_pairs={{16,0},{20,4},{24,8},{28,12},{32,16},{36,20},{40,24},{44,28},{48,3... | collective-permute-start | bytes 393224 | tf_op jit(solution)/shard_map/ppermute | solution.py:309
  164.4 12.8 %collective-permute-start.9 = (bf16[128,512]{1,0:T(8,128)(2,1)S(1)}, bf16[128,512]{1,0:T(8,128)(2,1)S(1)}, u32[]{:S(2)}, u32[]{:S(2)}) collective-permute-start(bf16[128,512]{1,0:T(8,128)(2,1)S(1)} %get-tuple-element.47), channel_id=1, source_target_pairs={{0,16},{4,20},{8,24},{12,28},{16,32},{20,36},{24,40},{28,44},{32,4... | collective-permute-start | bytes 393224 | tf_op jit(solution)/shard_map/ppermute | solution.py:309
  172.6 19.3 %collective-permute-start.11 = (f32[128,512]{1,0:T(8,128)S(1)}, f32[128,512]{1,0:T(8,128)S(1)}, u32[]{:S(2)}, u32[]{:S(2)}) collective-permute-start(f32[128,512]{1,0:T(8,128)S(1)} %get-tuple-element.49), channel_id=1, source_target_pairs={{16,0},{20,4},{24,8},{28,12},{32,16},{36,20},{40,24},{44,28},{48,3... | collective-permute-start | bytes 786440 | tf_op jit(solution)/shard_map/ppermute | solution.py:309
where the time goes:
time: 193 us
  starting transfers between devices  62.3 us (32%)
  Pallas kernels  55.9 us (29%)
  waiting for transfers between devices  55.5 us (29%)
  blocking collectives  11.2 us (6%)
  local copies, waits for them, and re-layouts  5.36 us (3%)
    ppermute x12, waiting for transfers between devices, passed_along(): return lax.ppermute(block, axis, route)  44.4 us
    ppermute x12, starting transfers between devices, passed_along(): return lax.ppermute(block, axis, route)  42.5 us
    pallas_call x3, Pallas kernels, inverse(): pl.pallas_call(functools.partial(inverse_kernel, with_rows), out_shape=ou...  42.1 us
    all_to_all x4, starting transfers between devices, exchanged(): return lax.all_to_all(blocks, 'swath', 0, 0, tiled=True)  19.8 us
    all_to_all x1, blocking collectives, exchanged(): return lax.all_to_all(blocks, 'swath', 0, 0, tiled=True)  11.2 us
    all_to_all x4, waiting for transfers between devices, exchanged(): return lax.all_to_all(blocks, 'swath', 0, 0, tiled=True)  11.1 us
    pallas_call x2, Pallas kernels, coupled(): pl.pallas_call(coupling_kernel, out_shape=jax.ShapeDtypeStruct(x.shape, f...  5.03 us
    unnamed x11, local copies, waits for them, and re-layouts  4.19 us
  transfers between devices with their start and end apart: 16, of which 9 were waited for; matrix products, arithmetic and copies ran while one was open for 0% of the time, Pallas kernels for 24%

commit v1 on v0

--- a/solution.py
+++ b/solution.py
@@ -52,13 +52,16 @@
         if stop < NB:
             after = a[stop : stop + WIDTH, :]
             weights = [jnp.broadcast_to(after[:, start + j : start + j + 1], (WIDTH, NB)) for j in range(WIDTH)]
+        scale = 1.0 / cols[0][:1, :]
         for j in range(WIDTH):
             c = cols[j]
-            scale = 1.0 / c[j : j + 1, :]
-            here = row == j
+            now, here = scale, row == j
+            if j + 1 < WIDTH:
+                pivot = cols[j + 1][j + 1 : j + 2, :] - (c[j + 1 : j + 2, :] * cols[j + 1][j : j + 1, :]) * now
+                scale = 1.0 / pivot
 
             def step(v):
-                t = v[j : j + 1, :] * scale
+                t = v[j : j + 1, :] * now
                 return jnp.where(here, t, v - c * t)
 
             for i in range(j + 1, WIDTH):
@@ -163,13 +166,15 @@
     ahead_ref[2 * rows :, :] = process_ref[...]
 
 
-def gram_kernel(own_ref, incoming_ref, out_ref):
+def gram_kernel(own_ref, incoming_ref, process_ref, out_ref, pairs_ref):
     both = jnp.concatenate([own_ref[...], incoming_ref[: own_ref.shape[0], :]], axis=0)
     g = mm(both, both, KK)
     for k in range(4):
         n, p, h = (k + 1) % 4, k % 2, HALF * (k // 2)
         out_ref[k, :NB, :] = g[k * NB : (k + 1) * NB, k * NB : (k + 1) * NB]
         out_ref[k, NB : 2 * NB, :] = g[k * NB : (k + 1) * NB, n * NB : (n + 1) * NB]
+        pairs_ref[k, :NB, :] = incoming_ref[own_ref.shape[0] :, :]
+        pairs_ref[k, NB:, :] = process_ref[...]
         out_ref[k, 2 * NB :, :] = g[p * NB + h : p * NB + h + HALF, (p + 2) * NB : (p + 3) * NB]
 
 
@@ -250,15 +255,22 @@
     )(sid, x, a, c)
 
 
-def terms_kernel(sid_ref, x_ref, a_ref, c_ref, *outs):
+def row_terms_kernel(sid_ref, x_ref, a_ref, c_ref, right_term, left_term):
     col = pl.multiple_of(sid_ref[0] * NB, NB)
-    lhs = jnp.concatenate([a_ref[pl.ds(col, NB), :].astype(f32), c_ref[:, pl.ds(col, NB)].astype(f32).T], axis=0)
+    lhs = jnp.concatenate([a_ref[pl.ds(col, NB), :], c_ref[:, pl.ds(col, NB)].T], axis=0)
     z = halves(split_dot(halves(lhs), halves(x_ref[...])))
-    top = z[0][:NB], z[1][:NB]
-    outs[0][...] = cross_dot(top, a_ref[...], MK).astype(bf16)
-    both = cross_dot(z, c_ref[...])
-    outs[1][...] = both[NB:].astype(bf16)
-    outs[2][...] = -both[:NB]
+    right_term[...] = cross_dot((z[0][:NB], z[1][:NB]), a_ref[...], MK).astype(bf16)
+    left_term[...] = cross_dot((z[0][NB:], z[1][NB:]), c_ref[...]).astype(bf16)
+
+
+def row_coupling_kernel(sid_ref, x_ref, a_ref, c_ref, n_ref):
+    rows = a_ref[pl.ds(pl.multiple_of(sid_ref[0] * NB, NB), NB), :]
+    z = split_dot(halves(rows), halves(x_ref[...]))
+    n_ref[...] = cross_dot(halves(z), c_ref[...])
+
+
+def negate_kernel(n_ref, out_ref):
+    out_ref[...] = -n_ref[...]
 
 
 def cross_dot(a, b, dims=KM):
@@ -267,17 +279,16 @@
     return split_dot(a, halves(b), dims)
 
 
-def terms(sid, x, a, c):
+def row_call(kernel, kinds, sid, x, a, c, name):
     size = x.shape[0]
-    term = jax.ShapeDtypeStruct((NB, size), bf16)
     return pl.pallas_call(
-        terms_kernel,
-        out_shape=(term, term, jax.ShapeDtypeStruct((NB, size), f32)),
+        kernel,
+        out_shape=[jax.ShapeDtypeStruct((NB, size), kind) for kind in kinds],
         in_specs=[SMEM] + [VMEM] * 3,
-        out_specs=(VMEM,) * 3,
-        compiler_params=PARAMS,
-        cost_estimate=pl.CostEstimate(flops=4 * size**3, bytes_accessed=16 * size * size, transcendentals=0),
-        name="terms",
+        out_specs=[VMEM] * len(kinds),
+        compiler_params=PARAMS,
+        cost_estimate=pl.CostEstimate(flops=8 * size**3, bytes_accessed=16 * size * size, transcendentals=0),
+        name=name,
     )(sid, x, a, c)
 
 
@@ -336,14 +347,14 @@
     incoming = passed_along(ahead, "tm", 1)
     cut = jax.ShapeDtypeStruct((2 * NB + HALF, NB), f32)
     cuts = jax.ShapeDtypeStruct((swaths,) + cut.shape, f32)
-    parts = pl.pallas_call(
+    parts, pairs = pl.pallas_call(
         gram_kernel,
-        out_shape=cuts,
-        in_specs=[VMEM] * 2,
-        out_specs=VMEM,
+        out_shape=(cuts, jax.ShapeDtypeStruct((swaths, 2 * row_count, size), bf16)),
+        in_specs=[VMEM] * 3,
+        out_specs=(VMEM, VMEM),
         compiler_params=PARAMS,
         name="gram",
-    )(own, incoming)
+    )(own, incoming, process[0])
     diag, copies = pl.pallas_call(
         start_kernel,
         out_shape=(cut, cuts),
@@ -352,8 +363,6 @@
         compiler_params=PARAMS,
         name="start",
     )(sids, exchanged(parts), process[0], incoming, prior_prec)
-    pair = jnp.concatenate([incoming[half:], process[0]], axis=0)
-    pairs = jnp.broadcast_to(pair[None], (swaths,) + pair.shape)
     copies, pairs = lax.optimization_barrier((copies, pairs))
     all_diag = exchanged(copies)
     pairs = exchanged(pairs)
@@ -364,10 +373,22 @@
     for level in range(LEVELS):
         distance = 2**level
         if level == LEVELS - 1:
-            out = terms(sids, x, a, c)
-            from_right = passed_along(out[0], "tm", -distance)
-            from_left = passed_along(out[1], "tm", distance)
-            coupling = passed_along(out[2], "tm", -distance)
+            (n,) = row_call(row_coupling_kernel, (f32,), sids, x, a, c, "row_coupling")
+            coupling = passed_along(n, "tm", -distance)
+            x, n = lax.optimization_barrier((x, n))
+            right_term, left_term = row_call(row_terms_kernel, (bf16, bf16), sids, x, a, c, "row_terms")
+            from_right = passed_along(right_term, "tm", -distance)
+            from_left = passed_along(left_term, "tm", distance)
+            coupling = pl.pallas_call(
+                negate_kernel,
+                out_shape=jax.ShapeDtypeStruct(coupling.shape, f32),
+                in_specs=[VMEM],
+                out_specs=VMEM,
+                compiler_params=PARAMS,
+                cost_estimate=pl.CostEstimate(flops=size * NB, bytes_accessed=8 * size * NB, transcendentals=0),
+                name="negate",
+            )(coupling)
+            rows, coupling = lax.optimization_barrier((rows, coupling))
             return ((rows - from_left.astype(f32) - from_right.astype(f32))[None], coupling[None])
         right_term, left_term = sliced_terms(sids, x, a, c)
         from_right = passed_along(right_term, "tm", -distance)

time: 193 us -> 186 us (0.964)
  the two profiles are of different devices: /device:TPU:242 before, /device:TPU:249 now
where the time goes in v1:
time: 186 us
  starting transfers between devices  68.7 us (37%)
  Pallas kernels  56.6 us (30%)
  waiting for transfers between devices  42.1 us (23%)
  blocking collectives  12.1 us (7%)
  local copies, waits for them, and re-layouts  3.68 us (2%)
    ppermute x12, starting transfers between devices, passed_along(): return lax.ppermute(block, axis, route)  52.3 us
    pallas_call x3, Pallas kernels, inverse(): pl.pallas_call(functools.partial(inverse_kernel, with_rows), out_shape=ou...  39.6 us
    ppermute x12, waiting for transfers between devices, passed_along(): return lax.ppermute(block, axis, route)  30.1 us
    all_to_all x4, starting transfers between devices, exchanged(): return lax.all_to_all(blocks, 'swath', 0, 0, tiled=True)  16.4 us
    all_to_all x1, blocking collectives, exchanged(): return lax.all_to_all(blocks, 'swath', 0, 0, tiled=True)  12.1 us
    all_to_all x4, waiting for transfers between devices, exchanged(): return lax.all_to_all(blocks, 'swath', 0, 0, tiled=True)  12 us
    pallas_call x2, Pallas kernels, row_call(): pl.pallas_call(kernel, out_shape=[jax.ShapeDtypeStruct((NB, size), kind)...  4.64 us
    pallas_call x2, Pallas kernels, coupled(): pl.pallas_call(coupling_kernel, out_shape=jax.ShapeDtypeStruct(x.shape, f...  4.06 us
  transfers between devices with their start and end apart: 16, of which 9 were waited for; matrix products, arithmetic and copies ran while one was open for 0% of the time, Pallas kernels for 25%

profile of v1, /device:TPU:249, one launch (start us, length us, event | category | flops | bytes accessed | tf_op | source)
XLA Modules:
  0.0 185.6 jit_solution(13598571246805213654)
XLA Ops:
  1.3 0.6 copy-done.6
  1.9 0.1 pad_add_fusion.ids_ref
  2.0 0.9 copy-done
  2.9 1.0 copy-done.2
  4.0 1.1 weigh.1
  5.0 5.0 %collective-permute-start = (bf16[384,512]{1,0:T(8,128)(2,1)S(1)}, bf16[384,512]{1,0:T(8,128)(2,1)S(1)}, u32[]{:S(2)}, u32[]{:S(2)}) collective-permute-start(bf16[384,512]{1,0:T(8,128)(2,1)S(1)} %get-tuple-element.31), channel_id=1, source_target_pairs={{0,4},{4,8},{8,12},{12,16},{16,20},{20,24},{24,28},{28,32},{32,36}... | collective-permute-start | bytes 1179656 | tf_op jit(solution)/shard_map/ppermute | solution.py:320
  10.0 4.7 %collective-permute-done.incoming_ref = bf16[384,512]{1,0:T(8,128)(2,1)S(1)} collective-permute-done((bf16[384,512]{1,0:T(8,128)(2,1)S(1)}, bf16[384,512]{1,0:T(8,128)(2,1)S(1)}, u32[]{:S(2)}, u32[]{:S(2)}) %collective-permute-start) | collective-permute-done | bytes 393248 | tf_op jit(solution)/shard_map/ppermute | solution.py:320
  14.7 1.7 gram.1
  16.4 4.2 %all-to-all-start = ((f32[4,320,128]{2,1,0:T(8,128)}), f32[4,320,128]{2,1,0:T(8,128)S(1)}, u32[]{:S(2)}, u32[]{:S(2)}) async-start(f32[4,320,128]{2,1,0:T(8,128)} %get-tuple-element.32), calls=%async_computation | async-start | bytes 1310720 | tf_op jit(solution)/shard_map/all_to_all | solution.py:324
  20.6 10.7 %all-to-all-done.parts_ref = f32[4,320,128]{2,1,0:T(8,128)S(1)} async-done(((f32[4,320,128]{2,1,0:T(8,128)}), f32[4,320,128]{2,1,0:T(8,128)S(1)}, u32[]{:S(2)}, u32[]{:S(2)}) %all-to-all-start) | async-done | bytes 655392 | tf_op jit(solution)/shard_map/all_to_all | solution.py:324
  31.2 0.1 start.1
  31.4 12.1 %all_to_all.25.g_ref = f32[4,320,128]{2,1,0:T(8,128)S(1)} all-to-all(f32[4,320,128]{2,1,0:T(8,128)S(1)} %get-tuple-element.36), channel_id=1, replica_groups=mesh['tm'=128,'swath'=4] {'swath'}, dimensions={0} | all-to-all | bytes 1310720 | tf_op jit(solution)/shard_map/all_to_all | solution.py:324
  43.5 3.5 %all-to-all-start.2 = ((bf16[4,256,512]{2,1,0:T(8,128)(2,1)}), bf16[4,256,512]{2,1,0:T(8,128)(2,1)S(1)}, u32[]{:S(2)}, u32[]{:S(2)}) async-start(bf16[4,256,512]{2,1,0:T(8,128)(2,1)} %get-tuple-element.37), calls=%async_computation.2 | async-start | bytes 2097152 | tf_op jit(solution)/shard_map/all_to_all | solution.py:324
  47.0 13.2 %inverse.3.x_ref = f32[512,512]{1,0:T(8,128)S(1)} custom-call(s32[1]{0:T(128)} %bitcast.sid_ref, f32[4,320,128]{2,1,0:T(8,128)S(1)} %all_to_all.25.g_ref), custom_call_target="tpu_custom_call" | custom-call | flops 8053063680 | bytes 2097152 | tf_op jit(solution)/shard_map/inverse/pallas_call | solution.py:131
  60.2 0.1 fusion
  60.3 1.3 sliced_terms.2
  61.6 4.7 %collective-permute-start.1 = (f32[320,128]{1,0:T(8,128)S(1)}, f32[320,128]{1,0:T(8,128)S(1)}, u32[]{:S(2)}, u32[]{:S(2)}) collective-permute-start(f32[320,128]{1,0:T(8,128)S(1)} %get-tuple-element.38), channel_id=1, source_target_pairs={{4,0},{8,4},{12,8},{16,12},{20,16},{24,20},{28,24},{32,28},{36,32}... | collective-permute-start | bytes 491528 | tf_op jit(solution)/shard_map/ppermute | solution.py:320
  66.4 4.1 %collective-permute-start.2 = (f32[320,128]{1,0:T(8,128)S(1)}, f32[320,128]{1,0:T(8,128)S(1)}, u32[]{:S(2)}, u32[]{:S(2)}) collective-permute-start(f32[320,128]{1,0:T(8,128)S(1)} %get-tuple-element.39), channel_id=1, source_target_pairs={{0,4},{4,8},{8,12},{12,16},{16,20},{20,24},{24,28},{28,32},{32,36}... | collective-permute-start | bytes 491528 | tf_op jit(solution)/shard_map/ppermute | solution.py:320
  70.5 2.3 %coupling.2 = f32[512,512]{1,0:T(8,128)} custom-call(f32[512,512]{1,0:T(8,128)S(1)} %inverse.3.x_ref, bf16[512,512]{1,0:T(8,128)(2,1)S(1)} %bitcast.15, bf16[512,512]{1,0:T(8,128)(2,1)S(1)} %bitcast.13), custom_call_target="tpu_custom_call" | custom-call | flops 1610612736 | bytes 4194304 | tf_op jit(solution)/shard_map/coupling/pallas_call | solution.py:306
  72.8 0.9 next.2
  73.7 4.2 %all-to-all-start.3 = ((f32[4,320,128]{2,1,0:T(8,128)}), f32[4,320,128]{2,1,0:T(8,128)S(1)}, u32[]{:S(2)}, u32[]{:S(2)}) async-start(f32[4,320,128]{2,1,0:T(8,128)} %get-tuple-element.43), calls=%async_computation.3 | async-start | bytes 1310720 | tf_op jit(solution)/shard_map/all_to_all | solution.py:324
  77.9 8.0 %collective-permute-start.3 = (f32[512,512]{1,0:T(8,128)}, f32[512,512]{1,0:T(8,128)S(1)}, u32[]{:S(2)}, u32[]{:S(2)}) collective-permute-start(f32[512,512]{1,0:T(8,128)} %coupling.2), channel_id=1, source_target_pairs={{0,4},{4,8},{8,12},{12,16},{16,20},{20,24},{24,28},{28,32},{32,36}... | collective-permute-start | bytes 3145736 | tf_op jit(solution)/shard_map/ppermute | solution.py:320
  85.9 1.9 %collective-permute-start.4 = (f32[512,512]{1,0:T(8,128)}, f32[512,512]{1,0:T(8,128)S(1)}, u32[]{:S(2)}, u32[]{:S(2)}) collective-permute-start(f32[512,512]{1,0:T(8,128)} %coupling.2), channel_id=1, source_target_pairs={{4,0},{8,4},{12,8},{16,12},{20,16},{24,20},{28,24},{32,28},{36,32}... | collective-permute-start | bytes 3145736 | tf_op jit(solution)/shard_map/ppermute | solution.py:320
  87.8 1.1 all-to-all-done.3.g_ref
  88.9 13.2 %inverse.4.x_ref = f32[512,512]{1,0:T(8,128)S(1)} custom-call(s32[1]{0:T(128)} %bitcast.sid_ref, f32[4,320,128]{2,1,0:T(8,128)S(1)} %all-to-all-done.3.g_ref), custom_call_target="tpu_custom_call" | custom-call | flops 8053063680 | bytes 2097152 | tf_op jit(solution)/shard_map/inverse/pallas_call | solution.py:131
  102.1 3.4 %collective-permute-done.4.c_ref = f32[512,512]{1,0:T(8,128)S(1)} collective-permute-done((f32[512,512]{1,0:T(8,128)}, f32[512,512]{1,0:T(8,128)S(1)}, u32[]{:S(2)}, u32[]{:S(2)}) %collective-permute-start.4) | collective-permute-done | bytes 1048608 | tf_op jit(solution)/shard_map/ppermute | solution.py:320
  105.5 1.5 sliced_terms.3
  107.1 1.9 %collective-permute-start.5 = (f32[320,128]{1,0:T(8,128)S(1)}, f32[320,128]{1,0:T(8,128)S(1)}, u32[]{:S(2)}, u32[]{:S(2)}) collective-permute-start(f32[320,128]{1,0:T(8,128)S(1)} %get-tuple-element.45), channel_id=1, source_target_pairs={{8,0},{12,4},{16,8},{20,12},{24,16},{28,20},{32,24},{36,28},{40,32... | collective-permute-start | bytes 491528 | tf_op jit(solution)/shard_map/ppermute | solution.py:320
  109.0 6.9 %collective-permute-start.6 = (f32[320,128]{1,0:T(8,128)S(1)}, f32[320,128]{1,0:T(8,128)S(1)}, u32[]{:S(2)}, u32[]{:S(2)}) collective-permute-start(f32[320,128]{1,0:T(8,128)S(1)} %get-tuple-element.46), channel_id=1, source_target_pairs={{0,8},{4,12},{8,16},{12,20},{16,24},{20,28},{24,32},{28,36},{32,40... | collective-permute-start | bytes 491528 | tf_op jit(solution)/shard_map/ppermute | solution.py:320
  115.9 1.8 coupling.3
  117.7 1.0 copy-done.4
  118.7 1.0 next.3
  119.6 4.5 %all-to-all-start.4 = ((f32[4,320,128]{2,1,0:T(8,128)}), f32[4,320,128]{2,1,0:T(8,128)S(1)}, u32[]{:S(2)}, u32[]{:S(2)}) async-start(f32[4,320,128]{2,1,0:T(8,128)} %get-tuple-element.49), calls=%async_computation.4 | async-start | bytes 1310720 | tf_op jit(solution)/shard_map/all_to_all | solution.py:324
  124.1 6.4 %collective-permute-start.7 = (f32[512,512]{1,0:T(8,128)S(1)}, f32[512,512]{1,0:T(8,128)S(1)}, u32[]{:S(2)}, u32[]{:S(2)}) collective-permute-start(f32[512,512]{1,0:T(8,128)S(1)} %copy-done.5), channel_id=1, source_target_pairs={{0,8},{4,12},{8,16},{12,20},{16,24},{20,28},{24,32},{28,36},{32,40... | collective-permute-start | bytes 3145736 | tf_op jit(solution)/shard_map/ppermute | solution.py:320
  130.5 1.9 %collective-permute-start.8 = (f32[512,512]{1,0:T(8,128)S(1)}, f32[512,512]{1,0:T(8,128)}, u32[]{:S(2)}, u32[]{:S(2)}) collective-permute-start(f32[512,512]{1,0:T(8,128)S(1)} %copy-done.5), channel_id=1, source_target_pairs={{8,0},{12,4},{16,8},{20,12},{24,16},{28,20},{32,24},{36,28},{40,32... | collective-permute-start | bytes 3145736 | tf_op jit(solution)/shard_map/ppermute | solution.py:320
  132.5 0.2 all-to-all-done.4.g_ref
  132.7 13.3 %inverse.5 = (f32[512,512]{1,0:T(8,128)S(1)}, f32[128,512]{1,0:T(8,128)S(1)}) custom-call(s32[1]{0:T(128)} %bitcast.sid_ref, f32[4,320,128]{2,1,0:T(8,128)S(1)} %all-to-all-done.4.g_ref), custom_call_target="tpu_custom_call" | custom-call | flops 8053063680 | bytes 2097152 | tf_op jit(solution)/shard_map/inverse/pallas_call | solution.py:131
  145.9 5.9 %collective-permute-done.7.a_ref = f32[512,512]{1,0:T(8,128)S(1)} collective-permute-done((f32[512,512]{1,0:T(8,128)S(1)}, f32[512,512]{1,0:T(8,128)S(1)}, u32[]{:S(2)}, u32[]{:S(2)}) %collective-permute-start.7) | collective-permute-done | bytes 1048608 | tf_op jit(solution)/shard_map/ppermute | solution.py:320
  151.8 7.5 %collective-permute-done.8.c_ref = f32[512,512]{1,0:T(8,128)} collective-permute-done((f32[512,512]{1,0:T(8,128)S(1)}, f32[512,512]{1,0:T(8,128)}, u32[]{:S(2)}, u32[]{:S(2)}) %collective-permute-start.8) | collective-permute-done | bytes 1048608 | tf_op jit(solution)/shard_map/ppermute | solution.py:320
  159.3 2.0 %row_coupling.1 = f32[128,512]{1,0:T(8,128)S(1)} custom-call(s32[1]{0:T(128)} %bitcast.sid_ref, f32[512,512]{1,0:T(8,128)S(1)} %get-tuple-element.54.x_ref, f32[512,512]{1,0:T(8,128)S(1)} %collective-permute-done.7.a_ref, f32[512,512]{1,0:T(8,128)} %collective-permute-done.8.c_ref), custom_call_target="tpu_custom_call" | custom-call | flops 1073741824 | bytes 4194304 | tf_op jit(solution)/shard_map/row_coupling/pallas_call | solution.py:284
  161.3 1.9 %collective-permute-start.9 = (f32[128,512]{1,0:T(8,128)S(1)}, f32[128,512]{1,0:T(8,128)S(1)}, u32[]{:S(2)}, u32[]{:S(2)}) collective-permute-start(f32[128,512]{1,0:T(8,128)S(1)} %row_coupling.1), channel_id=1, source_target_pairs={{16,0},{20,4},{24,8},{28,12},{32,16},{36,20},{40,24},{44,28},{48,3... | collective-permute-start | bytes 786440 | tf_op jit(solution)/shard_map/ppermute | solution.py:320
  163.3 2.6 %row_terms.1 = (bf16[128,512]{1,0:T(8,128)(2,1)S(1)}, bf16[128,512]{1,0:T(8,128)(2,1)S(1)}) custom-call(s32[1]{0:T(128)} %bitcast.sid_ref, f32[512,512]{1,0:T(8,128)S(1)} %get-tuple-element.54.x_ref, f32[512,512]{1,0:T(8,128)S(1)} %collective-permute-done.7.a_ref, f32[512,512]{1,0:T(8,128)} %collective-permute-done.8.c_ref), custom_call_target="tpu_custom_call" | custom-call | flops 1073741824 | bytes 4194304 | tf_op jit(solution)/shard_map/row_terms/pallas_call | solution.py:284
  165.9 1.9 %collective-permute-start.11 = (bf16[128,512]{1,0:T(8,128)(2,1)S(1)}, bf16[128,512]{1,0:T(8,128)(2,1)S(1)}, u32[]{:S(2)}, u32[]{:S(2)}) collective-permute-start(bf16[128,512]{1,0:T(8,128)(2,1)S(1)} %get-tuple-element.56), channel_id=1, source_target_pairs={{16,0},{20,4},{24,8},{28,12},{32,16},{36,20},{40,24},{44,28},{48,3... | collective-permute-start | bytes 393224 | tf_op jit(solution)/shard_map/ppermute | solution.py:320
  167.9 7.6 %collective-permute-start.10 = (bf16[128,512]{1,0:T(8,128)(2,1)S(1)}, bf16[128,512]{1,0:T(8,128)(2,1)S(1)}, u32[]{:S(2)}, u32[]{:S(2)}) collective-permute-start(bf16[128,512]{1,0:T(8,128)(2,1)S(1)} %get-tuple-element.55), channel_id=1, source_target_pairs={{0,16},{4,20},{8,24},{12,28},{16,32},{20,36},{24,40},{28,44},{32,4... | collective-permute-start | bytes 393224 | tf_op jit(solution)/shard_map/ppermute | solution.py:320
  175.5 6.6 %collective-permute-done.9.n_ref = f32[128,512]{1,0:T(8,128)S(1)} collective-permute-done((f32[128,512]{1,0:T(8,128)S(1)}, f32[128,512]{1,0:T(8,128)S(1)}, u32[]{:S(2)}, u32[]{:S(2)}) %collective-permute-start.9) | collective-permute-done | bytes 262176 | tf_op jit(solution)/shard_map/ppermute | solution.py:320
  182.0 0.7 negate.1
  182.8 2.0 %collective-permute-done.11 = bf16[128,512]{1,0:T(8,128)(2,1)S(1)} collective-permute-done((bf16[128,512]{1,0:T(8,128)(2,1)S(1)}, bf16[128,512]{1,0:T(8,128)(2,1)S(1)}, u32[]{:S(2)}, u32[]{:S(2)}) %collective-permute-start.11) | collective-permute-done | bytes 131104 | tf_op jit(solution)/shard_map/ppermute | solution.py:320
  184.8 0.7 subtract_bitcast_fusion
  (17 shorter events, 0.0 us)
Async XLA Ops:
  1.3 0.7 copy-start.6
  2.0 0.9 copy-start
  2.9 1.0 copy-start.2
  5.0 9.7 %collective-permute-start = (bf16[384,512]{1,0:T(8,128)(2,1)S(1)}, bf16[384,512]{1,0:T(8,128)(2,1)S(1)}, u32[]{:S(2)}, u32[]{:S(2)}) collective-permute-start(bf16[384,512]{1,0:T(8,128)(2,1)S(1)} %get-tuple-element.31), channel_id=1, source_target_pairs={{0,4},{4,8},{8,12},{12,16},{16,20},{20,24},{24,28},{28,32},{32,36}... | collective-permute-start | bytes 1179656 | tf_op jit(solution)/shard_map/ppermute | solution.py:320
  16.4 14.8 %copy-start.1 = (bf16[1,128,512]{2,1,0:T(8,128)(2,1)S(1)}, bf16[1,128,512]{2,1,0:T(8,128)(2,1)}, u32[]{:S(2)}) copy-start(bf16[1,128,512]{2,1,0:T(8,128)(2,1)} %param.6) | copy-start | bytes 393220
  16.4 14.8 %all-to-all-start = ((f32[4,320,128]{2,1,0:T(8,128)}), f32[4,320,128]{2,1,0:T(8,128)S(1)}, u32[]{:S(2)}, u32[]{:S(2)}) async-start(f32[4,320,128]{2,1,0:T(8,128)} %get-tuple-element.32), calls=%async_computation | async-start | bytes 1310720 | tf_op jit(solution)/shard_map/all_to_all | solution.py:324
  20.6 10.7 %copy-start.3 = (f32[1,128]{1,0:T(1,128)S(1)}, f32[1,128]{1,0:T(1,128)}, u32[]{:S(2)}) copy-start(f32[1,128]{1,0:T(1,128)} %prior_ref.1) | copy-start | bytes 1540
  43.5 16.7 %all-to-all-start.2 = ((bf16[4,256,512]{2,1,0:T(8,128)(2,1)}), bf16[4,256,512]{2,1,0:T(8,128)(2,1)S(1)}, u32[]{:S(2)}, u32[]{:S(2)}) async-start(bf16[4,256,512]{2,1,0:T(8,128)(2,1)} %get-tuple-element.37), calls=%async_computation.2 | async-start | bytes 2097152 | tf_op jit(solution)/shard_map/all_to_all | solution.py:324
  61.6 11.2 %collective-permute-start.1 = (f32[320,128]{1,0:T(8,128)S(1)}, f32[320,128]{1,0:T(8,128)S(1)}, u32[]{:S(2)}, u32[]{:S(2)}) collective-permute-start(f32[320,128]{1,0:T(8,128)S(1)} %get-tuple-element.38), channel_id=1, source_target_pairs={{4,0},{8,4},{12,8},{16,12},{20,16},{24,20},{28,24},{32,28},{36,32}... | collective-permute-start | bytes 491528 | tf_op jit(solution)/shard_map/ppermute | solution.py:320
  66.4 6.4 %collective-permute-start.2 = (f32[320,128]{1,0:T(8,128)S(1)}, f32[320,128]{1,0:T(8,128)S(1)}, u32[]{:S(2)}, u32[]{:S(2)}) collective-permute-start(f32[320,128]{1,0:T(8,128)S(1)} %get-tuple-element.39), channel_id=1, source_target_pairs={{0,4},{4,8},{8,12},{12,16},{16,20},{20,24},{24,28},{28,32},{32,36}... | collective-permute-start | bytes 491528 | tf_op jit(solution)/shard_map/ppermute | solution.py:320
  73.7 15.2 %all-to-all-start.3 = ((f32[4,320,128]{2,1,0:T(8,128)}), f32[4,320,128]{2,1,0:T(8,128)S(1)}, u32[]{:S(2)}, u32[]{:S(2)}) async-start(f32[4,320,128]{2,1,0:T(8,128)} %get-tuple-element.43), calls=%async_computation.3 | async-start | bytes 1310720 | tf_op jit(solution)/shard_map/all_to_all | solution.py:324
  77.9 24.2 %collective-permute-start.3 = (f32[512,512]{1,0:T(8,128)}, f32[512,512]{1,0:T(8,128)S(1)}, u32[]{:S(2)}, u32[]{:S(2)}) collective-permute-start(f32[512,512]{1,0:T(8,128)} %coupling.2), channel_id=1, source_target_pairs={{0,4},{4,8},{8,12},{12,16},{16,20},{20,24},{24,28},{28,32},{32,36}... | collective-permute-start | bytes 3145736 | tf_op jit(solution)/shard_map/ppermute | solution.py:320
  85.9 19.6 %collective-permute-start.4 = (f32[512,512]{1,0:T(8,128)}, f32[512,512]{1,0:T(8,128)S(1)}, u32[]{:S(2)}, u32[]{:S(2)}) collective-permute-start(f32[512,512]{1,0:T(8,128)} %coupling.2), channel_id=1, source_target_pairs={{4,0},{8,4},{12,8},{16,12},{20,16},{24,20},{28,24},{32,28},{36,32}... | collective-permute-start | bytes 3145736 | tf_op jit(solution)/shard_map/ppermute | solution.py:320
  107.1 11.6 %collective-permute-start.5 = (f32[320,128]{1,0:T(8,128)S(1)}, f32[320,128]{1,0:T(8,128)S(1)}, u32[]{:S(2)}, u32[]{:S(2)}) collective-permute-start(f32[320,128]{1,0:T(8,128)S(1)} %get-tuple-element.45), channel_id=1, source_target_pairs={{8,0},{12,4},{16,8},{20,12},{24,16},{28,20},{32,24},{36,28},{40,32... | collective-permute-start | bytes 491528 | tf_op jit(solution)/shard_map/ppermute | solution.py:320
  109.0 9.7 %collective-permute-start.6 = (f32[320,128]{1,0:T(8,128)S(1)}, f32[320,128]{1,0:T(8,128)S(1)}, u32[]{:S(2)}, u32[]{:S(2)}) collective-permute-start(f32[320,128]{1,0:T(8,128)S(1)} %get-tuple-element.46), channel_id=1, source_target_pairs={{0,8},{4,12},{8,16},{12,20},{16,24},{20,28},{24,32},{28,36},{32,40... | collective-permute-start | bytes 491528 | tf_op jit(solution)/shard_map/ppermute | solution.py:320
  117.7 1.0 copy-start.4
  118.6 5.5 %copy-start.5 = (f32[512,512]{1,0:T(8,128)S(1)}, f32[512,512]{1,0:T(8,128)}, u32[]{:S(2)}) copy-start(f32[512,512]{1,0:T(8,128)} %copy-done.4) | copy-start | bytes 3145732
  119.6 13.1 %all-to-all-start.4 = ((f32[4,320,128]{2,1,0:T(8,128)}), f32[4,320,128]{2,1,0:T(8,128)S(1)}, u32[]{:S(2)}, u32[]{:S(2)}) async-start(f32[4,320,128]{2,1,0:T(8,128)} %get-tuple-element.49), calls=%async_computation.4 | async-start | bytes 1310720 | tf_op jit(solution)/shard_map/all_to_all | solution.py:324
  124.1 27.7 %collective-permute-start.7 = (f32[512,512]{1,0:T(8,128)S(1)}, f32[512,512]{1,0:T(8,128)S(1)}, u32[]{:S(2)}, u32[]{:S(2)}) collective-permute-start(f32[512,512]{1,0:T(8,128)S(1)} %copy-done.5), channel_id=1, source_target_pairs={{0,8},{4,12},{8,16},{12,20},{16,24},{20,28},{24,32},{28,36},{32,40... | collective-permute-start | bytes 3145736 | tf_op jit(solution)/shard_map/ppermute | solution.py:320
  130.5 28.8 %collective-permute-start.8 = (f32[512,512]{1,0:T(8,128)S(1)}, f32[512,512]{1,0:T(8,128)}, u32[]{:S(2)}, u32[]{:S(2)}) collective-permute-start(f32[512,512]{1,0:T(8,128)S(1)} %copy-done.5), channel_id=1, source_target_pairs={{8,0},{12,4},{16,8},{20,12},{24,16},{28,20},{32,24},{36,28},{40,32... | collective-permute-start | bytes 3145736 | tf_op jit(solution)/shard_map/ppermute | solution.py:320
  161.3 20.7 %collective-permute-start.9 = (f32[128,512]{1,0:T(8,128)S(1)}, f32[128,512]{1,0:T(8,128)S(1)}, u32[]{:S(2)}, u32[]{:S(2)}) collective-permute-start(f32[128,512]{1,0:T(8,128)S(1)} %row_coupling.1), channel_id=1, source_target_pairs={{16,0},{20,4},{24,8},{28,12},{32,16},{36,20},{40,24},{44,28},{48,3... | collective-permute-start | bytes 786440 | tf_op jit(solution)/shard_map/ppermute | solution.py:320
  165.9 18.9 %collective-permute-start.11 = (bf16[128,512]{1,0:T(8,128)(2,1)S(1)}, bf16[128,512]{1,0:T(8,128)(2,1)S(1)}, u32[]{:S(2)}, u32[]{:S(2)}) collective-permute-start(bf16[128,512]{1,0:T(8,128)(2,1)S(1)} %get-tuple-element.56), channel_id=1, source_target_pairs={{16,0},{20,4},{24,8},{28,12},{32,16},{36,20},{40,24},{44,28},{48,3... | collective-permute-start | bytes 393224 | tf_op jit(solution)/shard_map/ppermute | solution.py:320
  167.9 16.9 %collective-permute-start.10 = (bf16[128,512]{1,0:T(8,128)(2,1)S(1)}, bf16[128,512]{1,0:T(8,128)(2,1)S(1)}, u32[]{:S(2)}, u32[]{:S(2)}) collective-permute-start(bf16[128,512]{1,0:T(8,128)(2,1)S(1)} %get-tuple-element.55), channel_id=1, source_target_pairs={{0,16},{4,20},{8,24},{12,28},{16,32},{20,36},{24,40},{28,44},{32,4... | collective-permute-start | bytes 393224 | tf_op jit(solution)/shard_map/ppermute | solution.py:320

commit v2 on v1

--- a/solution.py
+++ b/solution.py
@@ -13,6 +13,7 @@
 f32, bf16 = jnp.float32, jnp.bfloat16
 VMEM = pl.BlockSpec(memory_space=pltpu.VMEM)
 SMEM = pl.BlockSpec(memory_space=pltpu.SMEM)
+HBM = pl.BlockSpec(memory_space=pltpu.HBM)
 PARAMS = pltpu.CompilerParams(vmem_limit_bytes=48 * 2**20)
 KK, KM, MK = ((0,), (0,)), ((1,), (0,)), ((1,), (1,))
 
@@ -135,17 +136,24 @@
         out_specs=[VMEM] * len(outs),
         scratch_shapes=[pltpu.VMEM((size, NB), f32)],
         compiler_params=PARAMS,
-        cost_estimate=pl.CostEstimate(flops=60 * size**3, bytes_accessed=8 * size * size, transcendentals=0),
+        cost_estimate=pl.CostEstimate(flops=40*size**3 if with_rows else 60 * size**3, bytes_accessed=8 * size * size, transcendentals=0),
         name="inverse",
     )(sid, g)
 
 
-def weigh_kernel(total_slots, ids_ref, design_ref, process_ref, own_ref, ahead_ref):
+def weigh_kernel(total_slots, counts_ref, routes_ref, design_hbm, process_hbm, own_ref, ahead_ref, design_ref, process_ref, sems):
     rows = own_ref.shape[0] // 2
-    me, live_count = ids_ref[0], ids_ref[1]
+    loads = [
+        pltpu.make_async_copy(design_hbm.at[0], design_ref, sems.at[0]),
+        pltpu.make_async_copy(process_hbm.at[0], process_ref, sems.at[1]),
+    ]
+    for load in loads:
+        load.start()
+    me, live_count = lax.axis_index("tm"), counts_ref[0, 0]
+    loads[0].wait()
     own_seen = jnp.int32(0)
     for r in range(4):
-        target = ids_ref[2 + r]
+        target = routes_ref[0, r]
         is_own = target == me
         live = (r < live_count) & (is_own | (target == me + 1))
         h = design_ref[r * rows : (r + 1) * rows, :].astype(f32)
@@ -163,6 +171,7 @@
             ahead_ref[pl.ds(jnp.minimum(ahead_seen, 1) * rows, rows), :] = w
 
         own_seen = own_seen + jnp.where(is_own, 1, 0)
+    loads[1].wait()
     ahead_ref[2 * rows :, :] = process_ref[...]
 
 
@@ -327,10 +336,8 @@
 def shards(design, process, prior_prec, routes, counts):
     row_count, size = process.shape[1:]
     swaths = lax.axis_size("swath")
-    me = lax.axis_index("tm")
     sid = lax.axis_index("swath")
     total_slots = design.shape[1] * swaths
-    ids = jnp.concatenate([me[None].astype(jnp.int32), counts[0], routes[0]])
     sids = sid[None].astype(jnp.int32)
     half = design.shape[1] // 2
     own, ahead = pl.pallas_call(
@@ -339,11 +346,12 @@
             jax.ShapeDtypeStruct((half, size), bf16),
             jax.ShapeDtypeStruct((half + row_count, size), bf16),
         ),
-        in_specs=[SMEM] + [VMEM] * 2,
+        in_specs=[SMEM, SMEM, HBM, HBM],
         out_specs=(VMEM, VMEM),
-        compiler_params=PARAMS,
+        scratch_shapes=[pltpu.VMEM((design.shape[1], size), bf16), pltpu.VMEM((row_count, size), bf16), pltpu.SemaphoreType.DMA((2,))],
+        compiler_params=pltpu.CompilerParams(vmem_limit_bytes=63 * 2**20),
         name="weigh",
-    )(ids, design[0], process[0])
+    )(counts, routes, design, process)
     incoming = passed_along(ahead, "tm", 1)
     cut = jax.ShapeDtypeStruct((2 * NB + HALF, NB), f32)
     cuts = jax.ShapeDtypeStruct((swaths,) + cut.shape, f32)
@@ -391,10 +399,11 @@
             rows, coupling = lax.optimization_barrier((rows, coupling))
             return ((rows - from_left.astype(f32) - from_right.astype(f32))[None], coupling[None])
         right_term, left_term = sliced_terms(sids, x, a, c)
+        x, right_term, left_term = lax.optimization_barrier((x, right_term, left_term))
         from_right = passed_along(right_term, "tm", -distance)
         from_left = passed_along(left_term, "tm", distance)
         n = coupled(x, a, c)
-        from_right, from_left, n = lax.optimization_barrier((from_right, from_left, n))
+        from_right, from_left, _ = lax.optimization_barrier((from_right, from_left, n))
         diag, copies = pl.pallas_call(
             next_kernel,
             out_shape=(cut, cuts),

time: 186 us -> 177 us (0.952)
  the two profiles are of different devices: /device:TPU:249 before, /device:TPU:251 now
where the time goes in v2:
time: 177 us; the launch traced here: 176 us
  starting transfers between devices  62.7 us (35%)
  Pallas kernels  56.3 us (32%)
  waiting for transfers between devices  30.3 us (17%)
  blocking collectives  24 us (14%)
    ppermute x12, starting transfers between devices, passed_along(): return lax.ppermute(block, axis, route)  49.5 us
    pallas_call x3, Pallas kernels, inverse(): pl.pallas_call(functools.partial(inverse_kernel, with_rows), out_shape=ou...  39.6 us
    all_to_all x2, blocking collectives, exchanged(): return lax.all_to_all(blocks, 'swath', 0, 0, tiled=True)  24 us
    ppermute x12, waiting for transfers between devices, passed_along(): return lax.ppermute(block, axis, route)  20.7 us
    all_to_all x3, starting transfers between devices, exchanged(): return lax.all_to_all(blocks, 'swath', 0, 0, tiled=True)  13.2 us
    all_to_all x3, waiting for transfers between devices, exchanged(): return lax.all_to_all(blocks, 'swath', 0, 0, tiled=True)  9.58 us
    pallas_call x2, Pallas kernels, coupled(): pl.pallas_call(coupling_kernel, out_shape=jax.ShapeDtypeStruct(x.shape, f...  4.07 us
  transfers between devices with their start and end apart: 15, of which 5 were waited for; matrix products, arithmetic and copies ran while one was open for 0% of the time, Pallas kernels for 26%

profile of v2, /device:TPU:251, one launch (start us, length us, event | category | flops | bytes accessed | tf_op | source)
XLA Modules:
  0.0 176.5 jit_solution(99758364582126920)
XLA Ops:
  1.3 3.2 %weigh.1 = (bf16[256,512]{1,0:T(8,128)(2,1)}, bf16[384,512]{1,0:T(8,128)(2,1)}) custom-call(s32[1,1]{1,0:T(1,128)S(6)} %copy.7.counts_ref, s32[1,4]{1,0:T(1,128)} %routes_ref.1, bf16[1,512,512]{2,1,0:T(8,128)(2,1)} %design_hbm.1, bf16[1,128,512]{2,1,0:T(8,128)(2,1)} %process_hbm.1), custom_call_target="tpu_custom_call" | custom-call | tf_op jit(solution)/shard_map/weigh/pallas_call | solution.py:343
  4.5 5.0 %collective-permute-start = (bf16[384,512]{1,0:T(8,128)(2,1)}, bf16[384,512]{1,0:T(8,128)(2,1)S(1)}, u32[]{:S(2)}, u32[]{:S(2)}) collective-permute-start(bf16[384,512]{1,0:T(8,128)(2,1)} %get-tuple-element.35), channel_id=1, source_target_pairs={{0,4},{4,8},{8,12},{12,16},{16,20},{20,24},{24,28},{28,32},{32,36}... | collective-permute-start | bytes 1179656 | tf_op jit(solution)/shard_map/ppermute | solution.py:329
  9.5 5.0 %collective-permute-done.incoming_ref = bf16[384,512]{1,0:T(8,128)(2,1)S(1)} collective-permute-done((bf16[384,512]{1,0:T(8,128)(2,1)}, bf16[384,512]{1,0:T(8,128)(2,1)S(1)}, u32[]{:S(2)}, u32[]{:S(2)}) %collective-permute-start) | collective-permute-done | bytes 393248 | tf_op jit(solution)/shard_map/ppermute | solution.py:329
  14.5 0.9 copy-done.1
  15.5 1.7 gram.1
  17.2 4.3 %all-to-all-start = ((f32[4,320,128]{2,1,0:T(8,128)}), f32[4,320,128]{2,1,0:T(8,128)S(1)}, u32[]{:S(2)}, u32[]{:S(2)}) async-start(f32[4,320,128]{2,1,0:T(8,128)} %get-tuple-element.36), calls=%async_computation | async-start | bytes 1310720 | tf_op jit(solution)/shard_map/all_to_all | solution.py:333
  21.4 9.6 %all-to-all-done.parts_ref = f32[4,320,128]{2,1,0:T(8,128)S(1)} async-done(((f32[4,320,128]{2,1,0:T(8,128)}), f32[4,320,128]{2,1,0:T(8,128)S(1)}, u32[]{:S(2)}, u32[]{:S(2)}) %all-to-all-start) | async-done | bytes 655392 | tf_op jit(solution)/shard_map/all_to_all | solution.py:333
  31.0 0.1 start.1
  31.2 12.2 %all_to_all.25.g_ref = f32[4,320,128]{2,1,0:T(8,128)S(1)} all-to-all(f32[4,320,128]{2,1,0:T(8,128)S(1)} %get-tuple-element.40), channel_id=1, replica_groups=mesh['tm'=128,'swath'=4] {'swath'}, dimensions={0} | all-to-all | bytes 1310720 | tf_op jit(solution)/shard_map/all_to_all | solution.py:333
  43.4 4.7 %all-to-all-start.2 = ((bf16[4,256,512]{2,1,0:T(8,128)(2,1)}), bf16[4,256,512]{2,1,0:T(8,128)(2,1)S(1)}, u32[]{:S(2)}, u32[]{:S(2)}) async-start(bf16[4,256,512]{2,1,0:T(8,128)(2,1)} %get-tuple-element.41), calls=%async_computation.2 | async-start | bytes 2097152 | tf_op jit(solution)/shard_map/all_to_all | solution.py:333
  48.1 13.2 %inverse.3.x_ref = f32[512,512]{1,0:T(8,128)S(1)} custom-call(s32[1]{0:T(128)} %bitcast.sid_ref, f32[4,320,128]{2,1,0:T(8,128)S(1)} %all_to_all.25.g_ref), custom_call_target="tpu_custom_call" | custom-call | flops 8053063680 | bytes 2097152 | tf_op jit(solution)/shard_map/inverse/pallas_call | solution.py:132
  61.3 0.0 all-to-all-done.2
  61.3 0.1 fusion
  61.4 1.3 sliced_terms.2
  62.7 4.2 %collective-permute-start.1 = (f32[320,128]{1,0:T(8,128)S(1)}, f32[320,128]{1,0:T(8,128)S(1)}, u32[]{:S(2)}, u32[]{:S(2)}) collective-permute-start(f32[320,128]{1,0:T(8,128)S(1)} %get-tuple-element.44), channel_id=1, source_target_pairs={{4,0},{8,4},{12,8},{16,12},{20,16},{24,20},{28,24},{32,28},{36,32}... | collective-permute-start | bytes 491528 | tf_op jit(solution)/shard_map/ppermute | solution.py:329
  66.9 4.7 %collective-permute-start.2 = (f32[320,128]{1,0:T(8,128)S(1)}, f32[320,128]{1,0:T(8,128)S(1)}, u32[]{:S(2)}, u32[]{:S(2)}) collective-permute-start(f32[320,128]{1,0:T(8,128)S(1)} %get-tuple-element.45), channel_id=1, source_target_pairs={{0,4},{4,8},{8,12},{12,16},{16,20},{20,24},{24,28},{28,32},{32,36}... | collective-permute-start | bytes 491528 | tf_op jit(solution)/shard_map/ppermute | solution.py:329
  71.6 2.3 %coupling.2 = f32[512,512]{1,0:T(8,128)} custom-call(f32[512,512]{1,0:T(8,128)S(1)} %inverse.3.x_ref, bf16[512,512]{1,0:T(8,128)(2,1)S(1)} %bitcast.10, bf16[512,512]{1,0:T(8,128)(2,1)S(1)} %bitcast.8), custom_call_target="tpu_custom_call" | custom-call | flops 1610612736 | bytes 4194304 | tf_op jit(solution)/shard_map/coupling/pallas_call | solution.py:315
  73.8 0.0 collective-permute-done.1.right_ref
  73.8 0.0 collective-permute-done.2.left_ref
  73.8 0.9 next.2
  74.8 4.2 %all-to-all-start.3 = ((f32[4,320,128]{2,1,0:T(8,128)}), f32[4,320,128]{2,1,0:T(8,128)S(1)}, u32[]{:S(2)}, u32[]{:S(2)}) async-start(f32[4,320,128]{2,1,0:T(8,128)} %get-tuple-element.50), calls=%async_computation.3 | async-start | bytes 1310720 | tf_op jit(solution)/shard_map/all_to_all | solution.py:333
  79.0 8.2 %collective-permute-start.3 = (f32[512,512]{1,0:T(8,128)}, f32[512,512]{1,0:T(8,128)S(1)}, u32[]{:S(2)}, u32[]{:S(2)}) collective-permute-start(f32[512,512]{1,0:T(8,128)} %coupling.2), channel_id=1, source_target_pairs={{0,4},{4,8},{8,12},{12,16},{16,20},{20,24},{24,28},{28,32},{32,36}... | collective-permute-start | bytes 3145736 | tf_op jit(solution)/shard_map/ppermute | solution.py:329
  87.2 1.9 %collective-permute-start.4 = (f32[512,512]{1,0:T(8,128)}, f32[512,512]{1,0:T(8,128)S(1)}, u32[]{:S(2)}, u32[]{:S(2)}) collective-permute-start(f32[512,512]{1,0:T(8,128)} %coupling.2), channel_id=1, source_target_pairs={{4,0},{8,4},{12,8},{16,12},{20,16},{24,20},{28,24},{32,28},{36,32}... | collective-permute-start | bytes 3145736 | tf_op jit(solution)/shard_map/ppermute | solution.py:329
  89.2 0.0 all-to-all-done.3.g_ref
  89.2 13.2 %inverse.4.x_ref = f32[512,512]{1,0:T(8,128)S(1)} custom-call(s32[1]{0:T(128)} %bitcast.sid_ref, f32[4,320,128]{2,1,0:T(8,128)S(1)} %all-to-all-done.3.g_ref), custom_call_target="tpu_custom_call" | custom-call | flops 8053063680 | bytes 2097152 | tf_op jit(solution)/shard_map/inverse/pallas_call | solution.py:132
  102.4 0.0 collective-permute-done.3.a_ref
  102.4 4.5 %collective-permute-done.4.c_ref = f32[512,512]{1,0:T(8,128)S(1)} collective-permute-done((f32[512,512]{1,0:T(8,128)}, f32[512,512]{1,0:T(8,128)S(1)}, u32[]{:S(2)}, u32[]{:S(2)}) %collective-permute-start.4) | collective-permute-done | bytes 1048608 | tf_op jit(solution)/shard_map/ppermute | solution.py:329
  106.9 1.6 sliced_terms.3
  108.5 1.9 %collective-permute-start.5 = (f32[320,128]{1,0:T(8,128)S(1)}, f32[320,128]{1,0:T(8,128)S(1)}, u32[]{:S(2)}, u32[]{:S(2)}) collective-permute-start(f32[320,128]{1,0:T(8,128)S(1)} %get-tuple-element.53), channel_id=1, source_target_pairs={{8,0},{12,4},{16,8},{20,12},{24,16},{28,20},{32,24},{36,28},{40,32... | collective-permute-start | bytes 491528 | tf_op jit(solution)/shard_map/ppermute | solution.py:329
  110.4 6.7 %collective-permute-start.6 = (f32[320,128]{1,0:T(8,128)S(1)}, f32[320,128]{1,0:T(8,128)S(1)}, u32[]{:S(2)}, u32[]{:S(2)}) collective-permute-start(f32[320,128]{1,0:T(8,128)S(1)} %get-tuple-element.54), channel_id=1, source_target_pairs={{0,8},{4,12},{8,16},{12,20},{16,24},{20,28},{24,32},{28,36},{32,40... | collective-permute-start | bytes 491528 | tf_op jit(solution)/shard_map/ppermute | solution.py:329
  117.1 1.8 %coupling.3 = f32[512,512]{1,0:T(8,128)S(1)} custom-call(f32[512,512]{1,0:T(8,128)S(1)} %inverse.4.x_ref, f32[512,512]{1,0:T(8,128)S(1)} %collective-permute-done.3.a_ref, f32[512,512]{1,0:T(8,128)S(1)} %collective-permute-done.4.c_ref), custom_call_target="tpu_custom_call" | custom-call | flops 1610612736 | bytes 4194304 | tf_op jit(solution)/shard_map/coupling/pallas_call | solution.py:315
  118.9 2.1 %collective-permute-start.7 = (f32[512,512]{1,0:T(8,128)S(1)}, f32[512,512]{1,0:T(8,128)S(1)}, u32[]{:S(2)}, u32[]{:S(2)}) collective-permute-start(f32[512,512]{1,0:T(8,128)S(1)} %coupling.3), channel_id=1, source_target_pairs={{0,8},{4,12},{8,16},{12,20},{16,24},{20,28},{24,32},{28,36},{32,40... | collective-permute-start | bytes 3145736 | tf_op jit(solution)/shard_map/ppermute | solution.py:329
  121.0 3.4 %collective-permute-start.8 = (f32[512,512]{1,0:T(8,128)S(1)}, f32[512,512]{1,0:T(8,128)S(1)}, u32[]{:S(2)}, u32[]{:S(2)}) collective-permute-start(f32[512,512]{1,0:T(8,128)S(1)} %coupling.3), channel_id=1, source_target_pairs={{8,0},{12,4},{16,8},{20,12},{24,16},{28,20},{32,24},{36,28},{40,32... | collective-permute-start | bytes 3145736 | tf_op jit(solution)/shard_map/ppermute | solution.py:329
  124.4 0.0 collective-permute-done.5.right_ref
  124.4 0.7 next.3
  125.1 11.7 %all_to_all.26.g_ref = f32[4,320,128]{2,1,0:T(8,128)S(1)} all-to-all(f32[4,320,128]{2,1,0:T(8,128)S(1)} %get-tuple-element.58), channel_id=1, replica_groups=mesh['tm'=128,'swath'=4] {'swath'}, dimensions={0} | all-to-all | bytes 1310720 | tf_op jit(solution)/shard_map/all_to_all | solution.py:333
  136.8 13.3 %inverse.5 = (f32[512,512]{1,0:T(8,128)S(1)}, f32[128,512]{1,0:T(8,128)S(1)}) custom-call(s32[1]{0:T(128)} %bitcast.sid_ref, f32[4,320,128]{2,1,0:T(8,128)S(1)} %all_to_all.26.g_ref), custom_call_target="tpu_custom_call" | custom-call | flops 5368709120 | bytes 2097152 | tf_op jit(solution)/shard_map/inverse/pallas_call | solution.py:132
  150.1 0.0 collective-permute-done.8.c_ref
  150.1 0.8 row_coupling.1
  151.0 1.9 %collective-permute-start.9 = (f32[128,512]{1,0:T(8,128)S(1)}, f32[128,512]{1,0:T(8,128)S(1)}, u32[]{:S(2)}, u32[]{:S(2)}) collective-permute-start(f32[128,512]{1,0:T(8,128)S(1)} %row_coupling.1), channel_id=1, source_target_pairs={{16,0},{20,4},{24,8},{28,12},{32,16},{36,20},{40,24},{44,28},{48,3... | collective-permute-start | bytes 786440 | tf_op jit(solution)/shard_map/ppermute | solution.py:329
  152.9 1.5 row_terms.1
  154.3 1.9 %collective-permute-start.11 = (bf16[128,512]{1,0:T(8,128)(2,1)S(1)}, bf16[128,512]{1,0:T(8,128)(2,1)S(1)}, u32[]{:S(2)}, u32[]{:S(2)}) collective-permute-start(bf16[128,512]{1,0:T(8,128)(2,1)S(1)} %get-tuple-element.64), channel_id=1, source_target_pairs={{16,0},{20,4},{24,8},{28,12},{32,16},{36,20},{40,24},{44,28},{48,3... | collective-permute-start | bytes 393224 | tf_op jit(solution)/shard_map/ppermute | solution.py:329
  156.3 7.6 %collective-permute-start.10 = (bf16[128,512]{1,0:T(8,128)(2,1)S(1)}, bf16[128,512]{1,0:T(8,128)(2,1)S(1)}, u32[]{:S(2)}, u32[]{:S(2)}) collective-permute-start(bf16[128,512]{1,0:T(8,128)(2,1)S(1)} %get-tuple-element.63), channel_id=1, source_target_pairs={{0,16},{4,20},{8,24},{12,28},{16,32},{20,36},{24,40},{28,44},{32,4... | collective-permute-start | bytes 393224 | tf_op jit(solution)/shard_map/ppermute | solution.py:329
  163.9 7.9 %collective-permute-done.9.n_ref = f32[128,512]{1,0:T(8,128)S(1)} collective-permute-done((f32[128,512]{1,0:T(8,128)S(1)}, f32[128,512]{1,0:T(8,128)S(1)}, u32[]{:S(2)}, u32[]{:S(2)}) %collective-permute-start.9) | collective-permute-done | bytes 262176 | tf_op jit(solution)/shard_map/ppermute | solution.py:329
  171.7 0.7 negate.1
  172.5 3.3 %collective-permute-done.11 = bf16[128,512]{1,0:T(8,128)(2,1)S(1)} collective-permute-done((bf16[128,512]{1,0:T(8,128)(2,1)S(1)}, bf16[128,512]{1,0:T(8,128)(2,1)S(1)}, u32[]{:S(2)}, u32[]{:S(2)}) %collective-permute-start.11) | collective-permute-done | bytes 131104 | tf_op jit(solution)/shard_map/ppermute | solution.py:329
  175.7 0.0 collective-permute-done.10
  175.7 0.7 subtract_bitcast_fusion
  (7 shorter events, 0.0 us)
Async XLA Ops:
  1.3 13.2 %copy-start = (bf16[1,128,512]{2,1,0:T(8,128)(2,1)S(1)}, bf16[1,128,512]{2,1,0:T(8,128)(2,1)}, u32[]{:S(2)}) copy-start(bf16[1,128,512]{2,1,0:T(8,128)(2,1)} %process_hbm.1) | copy-start | bytes 393220
  4.5 10.0 %collective-permute-start = (bf16[384,512]{1,0:T(8,128)(2,1)}, bf16[384,512]{1,0:T(8,128)(2,1)S(1)}, u32[]{:S(2)}, u32[]{:S(2)}) collective-permute-start(bf16[384,512]{1,0:T(8,128)(2,1)} %get-tuple-element.35), channel_id=1, source_target_pairs={{0,4},{4,8},{8,12},{12,16},{16,20},{20,24},{24,28},{28,32},{32,36}... | collective-permute-start | bytes 1179656 | tf_op jit(solution)/shard_map/ppermute | solution.py:329
  14.5 1.0 copy-start.1
  17.2 13.8 %all-to-all-start = ((f32[4,320,128]{2,1,0:T(8,128)}), f32[4,320,128]{2,1,0:T(8,128)S(1)}, u32[]{:S(2)}, u32[]{:S(2)}) async-start(f32[4,320,128]{2,1,0:T(8,128)} %get-tuple-element.36), calls=%async_computation | async-start | bytes 1310720 | tf_op jit(solution)/shard_map/all_to_all | solution.py:333
  21.4 9.6 %copy-start.2 = (f32[1,128]{1,0:T(1,128)S(1)}, f32[1,128]{1,0:T(1,128)}, u32[]{:S(2)}) copy-start(f32[1,128]{1,0:T(1,128)} %prior_ref.1) | copy-start | bytes 1540
  43.4 17.9 %all-to-all-start.2 = ((bf16[4,256,512]{2,1,0:T(8,128)(2,1)}), bf16[4,256,512]{2,1,0:T(8,128)(2,1)S(1)}, u32[]{:S(2)}, u32[]{:S(2)}) async-start(bf16[4,256,512]{2,1,0:T(8,128)(2,1)} %get-tuple-element.41), calls=%async_computation.2 | async-start | bytes 2097152 | tf_op jit(solution)/shard_map/all_to_all | solution.py:333
  62.7 11.2 %collective-permute-start.1 = (f32[320,128]{1,0:T(8,128)S(1)}, f32[320,128]{1,0:T(8,128)S(1)}, u32[]{:S(2)}, u32[]{:S(2)}) collective-permute-start(f32[320,128]{1,0:T(8,128)S(1)} %get-tuple-element.44), channel_id=1, source_target_pairs={{4,0},{8,4},{12,8},{16,12},{20,16},{24,20},{28,24},{32,28},{36,32}... | collective-permute-start | bytes 491528 | tf_op jit(solution)/shard_map/ppermute | solution.py:329
  66.9 7.0 %collective-permute-start.2 = (f32[320,128]{1,0:T(8,128)S(1)}, f32[320,128]{1,0:T(8,128)S(1)}, u32[]{:S(2)}, u32[]{:S(2)}) collective-permute-start(f32[320,128]{1,0:T(8,128)S(1)} %get-tuple-element.45), channel_id=1, source_target_pairs={{0,4},{4,8},{8,12},{12,16},{16,20},{20,24},{24,28},{28,32},{32,36}... | collective-permute-start | bytes 491528 | tf_op jit(solution)/shard_map/ppermute | solution.py:329
  74.8 14.4 %all-to-all-start.3 = ((f32[4,320,128]{2,1,0:T(8,128)}), f32[4,320,128]{2,1,0:T(8,128)S(1)}, u32[]{:S(2)}, u32[]{:S(2)}) async-start(f32[4,320,128]{2,1,0:T(8,128)} %get-tuple-element.50), calls=%async_computation.3 | async-start | bytes 1310720 | tf_op jit(solution)/shard_map/all_to_all | solution.py:333
  79.0 23.4 %collective-permute-start.3 = (f32[512,512]{1,0:T(8,128)}, f32[512,512]{1,0:T(8,128)S(1)}, u32[]{:S(2)}, u32[]{:S(2)}) collective-permute-start(f32[512,512]{1,0:T(8,128)} %coupling.2), channel_id=1, source_target_pairs={{0,4},{4,8},{8,12},{12,16},{16,20},{20,24},{24,28},{28,32},{32,36}... | collective-permute-start | bytes 3145736 | tf_op jit(solution)/shard_map/ppermute | solution.py:329
  87.2 19.6 %collective-permute-start.4 = (f32[512,512]{1,0:T(8,128)}, f32[512,512]{1,0:T(8,128)S(1)}, u32[]{:S(2)}, u32[]{:S(2)}) collective-permute-start(f32[512,512]{1,0:T(8,128)} %coupling.2), channel_id=1, source_target_pairs={{4,0},{8,4},{12,8},{16,12},{20,16},{24,20},{28,24},{32,28},{36,32}... | collective-permute-start | bytes 3145736 | tf_op jit(solution)/shard_map/ppermute | solution.py:329
  108.5 15.9 %collective-permute-start.5 = (f32[320,128]{1,0:T(8,128)S(1)}, f32[320,128]{1,0:T(8,128)S(1)}, u32[]{:S(2)}, u32[]{:S(2)}) collective-permute-start(f32[320,128]{1,0:T(8,128)S(1)} %get-tuple-element.53), channel_id=1, source_target_pairs={{8,0},{12,4},{16,8},{20,12},{24,16},{28,20},{32,24},{36,28},{40,32... | collective-permute-start | bytes 491528 | tf_op jit(solution)/shard_map/ppermute | solution.py:329
  110.4 14.0 %collective-permute-start.6 = (f32[320,128]{1,0:T(8,128)S(1)}, f32[320,128]{1,0:T(8,128)S(1)}, u32[]{:S(2)}, u32[]{:S(2)}) collective-permute-start(f32[320,128]{1,0:T(8,128)S(1)} %get-tuple-element.54), channel_id=1, source_target_pairs={{0,8},{4,12},{8,16},{12,20},{16,24},{20,28},{24,32},{28,36},{32,40... | collective-permute-start | bytes 491528 | tf_op jit(solution)/shard_map/ppermute | solution.py:329
  118.9 31.2 %collective-permute-start.7 = (f32[512,512]{1,0:T(8,128)S(1)}, f32[512,512]{1,0:T(8,128)S(1)}, u32[]{:S(2)}, u32[]{:S(2)}) collective-permute-start(f32[512,512]{1,0:T(8,128)S(1)} %coupling.3), channel_id=1, source_target_pairs={{0,8},{4,12},{8,16},{12,20},{16,24},{20,28},{24,32},{28,36},{32,40... | collective-permute-start | bytes 3145736 | tf_op jit(solution)/shard_map/ppermute | solution.py:329
  121.0 29.1 %collective-permute-start.8 = (f32[512,512]{1,0:T(8,128)S(1)}, f32[512,512]{1,0:T(8,128)S(1)}, u32[]{:S(2)}, u32[]{:S(2)}) collective-permute-start(f32[512,512]{1,0:T(8,128)S(1)} %coupling.3), channel_id=1, source_target_pairs={{8,0},{12,4},{16,8},{20,12},{24,16},{28,20},{32,24},{36,28},{40,32... | collective-permute-start | bytes 3145736 | tf_op jit(solution)/shard_map/ppermute | solution.py:329
  151.0 20.8 %collective-permute-start.9 = (f32[128,512]{1,0:T(8,128)S(1)}, f32[128,512]{1,0:T(8,128)S(1)}, u32[]{:S(2)}, u32[]{:S(2)}) collective-permute-start(f32[128,512]{1,0:T(8,128)S(1)} %row_coupling.1), channel_id=1, source_target_pairs={{16,0},{20,4},{24,8},{28,12},{32,16},{36,20},{40,24},{44,28},{48,3... | collective-permute-start | bytes 786440 | tf_op jit(solution)/shard_map/ppermute | solution.py:329
  154.3 21.4 %collective-permute-start.11 = (bf16[128,512]{1,0:T(8,128)(2,1)S(1)}, bf16[128,512]{1,0:T(8,128)(2,1)S(1)}, u32[]{:S(2)}, u32[]{:S(2)}) collective-permute-start(bf16[128,512]{1,0:T(8,128)(2,1)S(1)} %get-tuple-element.64), channel_id=1, source_target_pairs={{16,0},{20,4},{24,8},{28,12},{32,16},{36,20},{40,24},{44,28},{48,3... | collective-permute-start | bytes 393224 | tf_op jit(solution)/shard_map/ppermute | solution.py:329
  156.3 19.5 %collective-permute-start.10 = (bf16[128,512]{1,0:T(8,128)(2,1)S(1)}, bf16[128,512]{1,0:T(8,128)(2,1)S(1)}, u32[]{:S(2)}, u32[]{:S(2)}) collective-permute-start(bf16[128,512]{1,0:T(8,128)(2,1)S(1)} %get-tuple-element.63), channel_id=1, source_target_pairs={{0,16},{4,20},{8,24},{12,28},{16,32},{20,36},{24,40},{28,44},{32,4... | collective-permute-start | bytes 393224 | tf_op jit(solution)/shard_map/ppermute | solution.py:329

commit v3 on v2

--- a/solution.py
+++ b/solution.py
@@ -53,13 +53,14 @@
         if stop < NB:
             after = a[stop : stop + WIDTH, :]
             weights = [jnp.broadcast_to(after[:, start + j : start + j + 1], (WIDTH, NB)) for j in range(WIDTH)]
-        scale = 1.0 / cols[0][:1, :]
+        units = [1.0 / cols[j][j : j + 1, :] for j in range(WIDTH)]
+        scale = jnp.ones((1, NB), f32)
         for j in range(WIDTH):
             c = cols[j]
-            now, here = scale, row == j
+            now, here = scale * units[j], row == j
             if j + 1 < WIDTH:
-                pivot = cols[j + 1][j + 1 : j + 2, :] - (c[j + 1 : j + 2, :] * cols[j + 1][j : j + 1, :]) * now
-                scale = 1.0 / pivot
+                pair = (c[j + 1 : j + 2, :] * units[j + 1]) * (cols[j + 1][j : j + 1, :] * units[j])
+                scale = 1.0 / (cols[j + 1][j + 1 : j + 2, :] * units[j + 1] - pair * scale)
 
             def step(v):
                 t = v[j : j + 1, :] * now
@@ -175,14 +176,18 @@
     ahead_ref[2 * rows :, :] = process_ref[...]
 
 
-def gram_kernel(own_ref, incoming_ref, process_ref, out_ref, pairs_ref):
-    both = jnp.concatenate([own_ref[...], incoming_ref[: own_ref.shape[0], :]], axis=0)
-    g = mm(both, both, KK)
+def own_gram_kernel(own_ref, g_ref):
+    g_ref[...] = mm(own_ref[...], own_ref[...], KK)
+
+
+def gram_kernel(g_ref, incoming_ref, process_ref, out_ref, pairs_ref):
+    half = incoming_ref.shape[0] - NB
+    g = g_ref[...] + mm(incoming_ref[:half, :], incoming_ref[:half, :], KK)
     for k in range(4):
         n, p, h = (k + 1) % 4, k % 2, HALF * (k // 2)
         out_ref[k, :NB, :] = g[k * NB : (k + 1) * NB, k * NB : (k + 1) * NB]
         out_ref[k, NB : 2 * NB, :] = g[k * NB : (k + 1) * NB, n * NB : (n + 1) * NB]
-        pairs_ref[k, :NB, :] = incoming_ref[own_ref.shape[0] :, :]
+        pairs_ref[k, :NB, :] = incoming_ref[half:, :]
         pairs_ref[k, NB:, :] = process_ref[...]
         out_ref[k, 2 * NB :, :] = g[p * NB + h : p * NB + h + HALF, (p + 2) * NB : (p + 3) * NB]
 
@@ -355,6 +360,15 @@
     incoming = passed_along(ahead, "tm", 1)
     cut = jax.ShapeDtypeStruct((2 * NB + HALF, NB), f32)
     cuts = jax.ShapeDtypeStruct((swaths,) + cut.shape, f32)
+    own_gram = pl.pallas_call(
+        own_gram_kernel,
+        out_shape=jax.ShapeDtypeStruct((size, size), f32),
+        in_specs=[VMEM],
+        out_specs=VMEM,
+        compiler_params=PARAMS,
+        cost_estimate=pl.CostEstimate(flops=2 * half * size**2, bytes_accessed=2 * 2**20, transcendentals=0),
+        name="own_gram",
+    )(own)
     parts, pairs = pl.pallas_call(
         gram_kernel,
         out_shape=(cuts, jax.ShapeDtypeStruct((swaths, 2 * row_count, size), bf16)),
@@ -362,7 +376,7 @@
         out_specs=(VMEM, VMEM),
         compiler_params=PARAMS,
         name="gram",
-    )(own, incoming, process[0])
+    )(own_gram, incoming, process[0])
     diag, copies = pl.pallas_call(
         start_kernel,
         out_shape=(cut, cuts),

time: 177 us -> 175 us (0.989)
  transfers between devices with their start and end apart: 15 -> 15, of which waited for: 5 -> 5; matrix products, arithmetic and copies ran while one was open for 0% -> 0% of each run, Pallas kernels for 26% -> 27%
where the time goes in v3:
time: 175 us
  starting transfers between devices  62.7 us (36%)
  Pallas kernels  55.7 us (32%)
  waiting for transfers between devices  29.2 us (17%)
  blocking collectives  23.8 us (14%)
    ppermute x12, starting transfers between devices, passed_along(): return lax.ppermute(block, axis, route)  49.5 us
    pallas_call x3, Pallas kernels, inverse(): pl.pallas_call(functools.partial(inverse_kernel, with_rows), out_shape=ou...  39 us
    all_to_all x2, blocking collectives, exchanged(): return lax.all_to_all(blocks, 'swath', 0, 0, tiled=True)  23.8 us
    ppermute x12, waiting for transfers between devices, passed_along(): return lax.ppermute(block, axis, route)  19.6 us
    all_to_all x3, starting transfers between devices, exchanged(): return lax.all_to_all(blocks, 'swath', 0, 0, tiled=True)  13.2 us
    all_to_all x3, waiting for transfers between devices, exchanged(): return lax.all_to_all(blocks, 'swath', 0, 0, tiled=True)  9.58 us
    pallas_call x2, Pallas kernels, coupled(): pl.pallas_call(coupling_kernel, out_shape=jax.ShapeDtypeStruct(x.shape, f...  4.07 us
  transfers between devices with their start and end apart: 15, of which 5 were waited for; matrix products, arithmetic and copies ran while one was open for 0% of the time, Pallas kernels for 27%

profile of v3, /device:TPU:251, one launch (start us, length us, event | category | flops | bytes accessed | tf_op | source)
XLA Modules:
  0.0 174.7 jit_solution(11859399719573510893)
XLA Ops:
  1.3 3.1 %weigh.1 = (bf16[256,512]{1,0:T(8,128)(2,1)}, bf16[384,512]{1,0:T(8,128)(2,1)}) custom-call(s32[1,1]{1,0:T(1,128)S(6)} %copy.7.counts_ref, s32[1,4]{1,0:T(1,128)} %routes_ref.1, bf16[1,512,512]{2,1,0:T(8,128)(2,1)} %design_hbm.1, bf16[1,128,512]{2,1,0:T(8,128)(2,1)} %process_hbm.1), custom_call_target="tpu_custom_call" | custom-call | tf_op jit(solution)/shard_map/weigh/pallas_call | solution.py:348
  4.4 5.0 %collective-permute-start = (bf16[384,512]{1,0:T(8,128)(2,1)}, bf16[384,512]{1,0:T(8,128)(2,1)S(1)}, u32[]{:S(2)}, u32[]{:S(2)}) collective-permute-start(bf16[384,512]{1,0:T(8,128)(2,1)} %get-tuple-element.35), channel_id=1, source_target_pairs={{0,4},{4,8},{8,12},{12,16},{16,20},{20,24},{24,28},{28,32},{32,36}... | collective-permute-start | bytes 1179656 | tf_op jit(solution)/shard_map/ppermute | solution.py:334
  9.4 0.0 copy-start.1
  9.4 0.9 copy-done.1
  10.3 0.3 own_gram.1.g_ref
  10.6 3.7 %collective-permute-done.incoming_ref = bf16[384,512]{1,0:T(8,128)(2,1)S(1)} collective-permute-done((bf16[384,512]{1,0:T(8,128)(2,1)}, bf16[384,512]{1,0:T(8,128)(2,1)S(1)}, u32[]{:S(2)}, u32[]{:S(2)}) %collective-permute-start) | collective-permute-done | bytes 393248 | tf_op jit(solution)/shard_map/ppermute | solution.py:334
  14.4 1.6 gram.1
  15.9 4.3 %all-to-all-start = ((f32[4,320,128]{2,1,0:T(8,128)}), f32[4,320,128]{2,1,0:T(8,128)S(1)}, u32[]{:S(2)}, u32[]{:S(2)}) async-start(f32[4,320,128]{2,1,0:T(8,128)} %get-tuple-element.36), calls=%async_computation | async-start | bytes 1310720 | tf_op jit(solution)/shard_map/all_to_all | solution.py:338
  20.2 9.6 %all-to-all-done.parts_ref = f32[4,320,128]{2,1,0:T(8,128)S(1)} async-done(((f32[4,320,128]{2,1,0:T(8,128)}), f32[4,320,128]{2,1,0:T(8,128)S(1)}, u32[]{:S(2)}, u32[]{:S(2)}) %all-to-all-start) | async-done | bytes 655392 | tf_op jit(solution)/shard_map/all_to_all | solution.py:338
  29.8 0.1 start.1
  29.9 12.2 %all_to_all.25.g_ref = f32[4,320,128]{2,1,0:T(8,128)S(1)} all-to-all(f32[4,320,128]{2,1,0:T(8,128)S(1)} %get-tuple-element.40), channel_id=1, replica_groups=mesh['tm'=128,'swath'=4] {'swath'}, dimensions={0} | all-to-all | bytes 1310720 | tf_op jit(solution)/shard_map/all_to_all | solution.py:338
  42.2 4.7 %all-to-all-start.2 = ((bf16[4,256,512]{2,1,0:T(8,128)(2,1)}), bf16[4,256,512]{2,1,0:T(8,128)(2,1)S(1)}, u32[]{:S(2)}, u32[]{:S(2)}) async-start(bf16[4,256,512]{2,1,0:T(8,128)(2,1)} %get-tuple-element.41), calls=%async_computation.2 | async-start | bytes 2097152 | tf_op jit(solution)/shard_map/all_to_all | solution.py:338
  46.8 13.0 %inverse.3.x_ref = f32[512,512]{1,0:T(8,128)S(1)} custom-call(s32[1]{0:T(128)} %bitcast.sid_ref, f32[4,320,128]{2,1,0:T(8,128)S(1)} %all_to_all.25.g_ref), custom_call_target="tpu_custom_call" | custom-call | flops 8053063680 | bytes 2097152 | tf_op jit(solution)/shard_map/inverse/pallas_call | solution.py:133
  59.8 0.0 all-to-all-done.2
  59.8 0.1 fusion
  60.0 1.3 sliced_terms.2
  61.3 4.2 %collective-permute-start.1 = (f32[320,128]{1,0:T(8,128)S(1)}, f32[320,128]{1,0:T(8,128)S(1)}, u32[]{:S(2)}, u32[]{:S(2)}) collective-permute-start(f32[320,128]{1,0:T(8,128)S(1)} %get-tuple-element.44), channel_id=1, source_target_pairs={{4,0},{8,4},{12,8},{16,12},{20,16},{24,20},{28,24},{32,28},{36,32}... | collective-permute-start | bytes 491528 | tf_op jit(solution)/shard_map/ppermute | solution.py:334
  65.5 4.7 %collective-permute-start.2 = (f32[320,128]{1,0:T(8,128)S(1)}, f32[320,128]{1,0:T(8,128)S(1)}, u32[]{:S(2)}, u32[]{:S(2)}) collective-permute-start(f32[320,128]{1,0:T(8,128)S(1)} %get-tuple-element.45), channel_id=1, source_target_pairs={{0,4},{4,8},{8,12},{12,16},{16,20},{20,24},{24,28},{28,32},{32,36}... | collective-permute-start | bytes 491528 | tf_op jit(solution)/shard_map/ppermute | solution.py:334
  70.2 2.3 %coupling.2 = f32[512,512]{1,0:T(8,128)} custom-call(f32[512,512]{1,0:T(8,128)S(1)} %inverse.3.x_ref, bf16[512,512]{1,0:T(8,128)(2,1)S(1)} %bitcast.10, bf16[512,512]{1,0:T(8,128)(2,1)S(1)} %bitcast.8), custom_call_target="tpu_custom_call" | custom-call | flops 1610612736 | bytes 4194304 | tf_op jit(solution)/shard_map/coupling/pallas_call | solution.py:320
  72.4 0.0 collective-permute-done.1.right_ref
  72.4 0.0 collective-permute-done.2.left_ref
  72.4 0.9 next.2
  73.3 4.3 %all-to-all-start.3 = ((f32[4,320,128]{2,1,0:T(8,128)}), f32[4,320,128]{2,1,0:T(8,128)S(1)}, u32[]{:S(2)}, u32[]{:S(2)}) async-start(f32[4,320,128]{2,1,0:T(8,128)} %get-tuple-element.50), calls=%async_computation.3 | async-start | bytes 1310720 | tf_op jit(solution)/shard_map/all_to_all | solution.py:338
  77.6 8.2 %collective-permute-start.3 = (f32[512,512]{1,0:T(8,128)}, f32[512,512]{1,0:T(8,128)S(1)}, u32[]{:S(2)}, u32[]{:S(2)}) collective-permute-start(f32[512,512]{1,0:T(8,128)} %coupling.2), channel_id=1, source_target_pairs={{0,4},{4,8},{8,12},{12,16},{16,20},{20,24},{24,28},{28,32},{32,36}... | collective-permute-start | bytes 3145736 | tf_op jit(solution)/shard_map/ppermute | solution.py:334
  85.8 1.9 %collective-permute-start.4 = (f32[512,512]{1,0:T(8,128)}, f32[512,512]{1,0:T(8,128)S(1)}, u32[]{:S(2)}, u32[]{:S(2)}) collective-permute-start(f32[512,512]{1,0:T(8,128)} %coupling.2), channel_id=1, source_target_pairs={{4,0},{8,4},{12,8},{16,12},{20,16},{24,20},{28,24},{32,28},{36,32}... | collective-permute-start | bytes 3145736 | tf_op jit(solution)/shard_map/ppermute | solution.py:334
  87.8 0.0 all-to-all-done.3.g_ref
  87.8 13.0 %inverse.4.x_ref = f32[512,512]{1,0:T(8,128)S(1)} custom-call(s32[1]{0:T(128)} %bitcast.sid_ref, f32[4,320,128]{2,1,0:T(8,128)S(1)} %all-to-all-done.3.g_ref), custom_call_target="tpu_custom_call" | custom-call | flops 8053063680 | bytes 2097152 | tf_op jit(solution)/shard_map/inverse/pallas_call | solution.py:133
  100.8 0.0 collective-permute-done.3.a_ref
  100.8 4.7 %collective-permute-done.4.c_ref = f32[512,512]{1,0:T(8,128)S(1)} collective-permute-done((f32[512,512]{1,0:T(8,128)}, f32[512,512]{1,0:T(8,128)S(1)}, u32[]{:S(2)}, u32[]{:S(2)}) %collective-permute-start.4) | collective-permute-done | bytes 1048608 | tf_op jit(solution)/shard_map/ppermute | solution.py:334
  105.5 1.6 sliced_terms.3
  107.1 1.9 %collective-permute-start.5 = (f32[320,128]{1,0:T(8,128)S(1)}, f32[320,128]{1,0:T(8,128)S(1)}, u32[]{:S(2)}, u32[]{:S(2)}) collective-permute-start(f32[320,128]{1,0:T(8,128)S(1)} %get-tuple-element.53), channel_id=1, source_target_pairs={{8,0},{12,4},{16,8},{20,12},{24,16},{28,20},{32,24},{36,28},{40,32... | collective-permute-start | bytes 491528 | tf_op jit(solution)/shard_map/ppermute | solution.py:334
  109.0 6.9 %collective-permute-start.6 = (f32[320,128]{1,0:T(8,128)S(1)}, f32[320,128]{1,0:T(8,128)S(1)}, u32[]{:S(2)}, u32[]{:S(2)}) collective-permute-start(f32[320,128]{1,0:T(8,128)S(1)} %get-tuple-element.54), channel_id=1, source_target_pairs={{0,8},{4,12},{8,16},{12,20},{16,24},{20,28},{24,32},{28,36},{32,40... | collective-permute-start | bytes 491528 | tf_op jit(solution)/shard_map/ppermute | solution.py:334
  115.8 1.8 %coupling.3 = f32[512,512]{1,0:T(8,128)S(1)} custom-call(f32[512,512]{1,0:T(8,128)S(1)} %inverse.4.x_ref, f32[512,512]{1,0:T(8,128)S(1)} %collective-permute-done.3.a_ref, f32[512,512]{1,0:T(8,128)S(1)} %collective-permute-done.4.c_ref), custom_call_target="tpu_custom_call" | custom-call | flops 1610612736 | bytes 4194304 | tf_op jit(solution)/shard_map/coupling/pallas_call | solution.py:320
  117.7 1.9 %collective-permute-start.7 = (f32[512,512]{1,0:T(8,128)S(1)}, f32[512,512]{1,0:T(8,128)S(1)}, u32[]{:S(2)}, u32[]{:S(2)}) collective-permute-start(f32[512,512]{1,0:T(8,128)S(1)} %coupling.3), channel_id=1, source_target_pairs={{0,8},{4,12},{8,16},{12,20},{16,24},{20,28},{24,32},{28,36},{32,40... | collective-permute-start | bytes 3145736 | tf_op jit(solution)/shard_map/ppermute | solution.py:334
  119.6 3.4 %collective-permute-start.8 = (f32[512,512]{1,0:T(8,128)S(1)}, f32[512,512]{1,0:T(8,128)S(1)}, u32[]{:S(2)}, u32[]{:S(2)}) collective-permute-start(f32[512,512]{1,0:T(8,128)S(1)} %coupling.3), channel_id=1, source_target_pairs={{8,0},{12,4},{16,8},{20,12},{24,16},{28,20},{32,24},{36,28},{40,32... | collective-permute-start | bytes 3145736 | tf_op jit(solution)/shard_map/ppermute | solution.py:334
  123.0 0.0 collective-permute-done.5.right_ref
  123.0 0.7 next.3
  123.7 11.6 %all_to_all.26.g_ref = f32[4,320,128]{2,1,0:T(8,128)S(1)} all-to-all(f32[4,320,128]{2,1,0:T(8,128)S(1)} %get-tuple-element.58), channel_id=1, replica_groups=mesh['tm'=128,'swath'=4] {'swath'}, dimensions={0} | all-to-all | bytes 1310720 | tf_op jit(solution)/shard_map/all_to_all | solution.py:338
  135.3 13.0 %inverse.5 = (f32[512,512]{1,0:T(8,128)S(1)}, f32[128,512]{1,0:T(8,128)S(1)}) custom-call(s32[1]{0:T(128)} %bitcast.sid_ref, f32[4,320,128]{2,1,0:T(8,128)S(1)} %all_to_all.26.g_ref), custom_call_target="tpu_custom_call" | custom-call | flops 5368709120 | bytes 2097152 | tf_op jit(solution)/shard_map/inverse/pallas_call | solution.py:133
  148.3 0.8 row_coupling.1
  149.1 1.9 %collective-permute-start.9 = (f32[128,512]{1,0:T(8,128)S(1)}, f32[128,512]{1,0:T(8,128)S(1)}, u32[]{:S(2)}, u32[]{:S(2)}) collective-permute-start(f32[128,512]{1,0:T(8,128)S(1)} %row_coupling.1), channel_id=1, source_target_pairs={{16,0},{20,4},{24,8},{28,12},{32,16},{36,20},{40,24},{44,28},{48,3... | collective-permute-start | bytes 786440 | tf_op jit(solution)/shard_map/ppermute | solution.py:334
  151.0 1.5 row_terms.1
  152.5 1.9 %collective-permute-start.11 = (bf16[128,512]{1,0:T(8,128)(2,1)S(1)}, bf16[128,512]{1,0:T(8,128)(2,1)S(1)}, u32[]{:S(2)}, u32[]{:S(2)}) collective-permute-start(bf16[128,512]{1,0:T(8,128)(2,1)S(1)} %get-tuple-element.64), channel_id=1, source_target_pairs={{16,0},{20,4},{24,8},{28,12},{32,16},{36,20},{40,24},{44,28},{48,3... | collective-permute-start | bytes 393224 | tf_op jit(solution)/shard_map/ppermute | solution.py:334
  154.4 7.6 %collective-permute-start.10 = (bf16[128,512]{1,0:T(8,128)(2,1)S(1)}, bf16[128,512]{1,0:T(8,128)(2,1)S(1)}, u32[]{:S(2)}, u32[]{:S(2)}) collective-permute-start(bf16[128,512]{1,0:T(8,128)(2,1)S(1)} %get-tuple-element.63), channel_id=1, source_target_pairs={{0,16},{4,20},{8,24},{12,28},{16,32},{20,36},{24,40},{28,44},{32,4... | collective-permute-start | bytes 393224 | tf_op jit(solution)/shard_map/ppermute | solution.py:334
  162.0 7.8 %collective-permute-done.9.n_ref = f32[128,512]{1,0:T(8,128)S(1)} collective-permute-done((f32[128,512]{1,0:T(8,128)S(1)}, f32[128,512]{1,0:T(8,128)S(1)}, u32[]{:S(2)}, u32[]{:S(2)}) %collective-permute-start.9) | collective-permute-done | bytes 262176 | tf_op jit(solution)/shard_map/ppermute | solution.py:334
  169.8 0.7 negate.1
  170.6 3.4 %collective-permute-done.11 = bf16[128,512]{1,0:T(8,128)(2,1)S(1)} collective-permute-done((bf16[128,512]{1,0:T(8,128)(2,1)S(1)}, bf16[128,512]{1,0:T(8,128)(2,1)S(1)}, u32[]{:S(2)}, u32[]{:S(2)}) %collective-permute-start.11) | collective-permute-done | bytes 131104 | tf_op jit(solution)/shard_map/ppermute | solution.py:334
  174.0 0.7 subtract_bitcast_fusion
  (8 shorter events, 0.0 us)
Async XLA Ops:
  4.4 10.0 %collective-permute-start = (bf16[384,512]{1,0:T(8,128)(2,1)}, bf16[384,512]{1,0:T(8,128)(2,1)S(1)}, u32[]{:S(2)}, u32[]{:S(2)}) collective-permute-start(bf16[384,512]{1,0:T(8,128)(2,1)} %get-tuple-element.35), channel_id=1, source_target_pairs={{0,4},{4,8},{8,12},{12,16},{16,20},{20,24},{24,28},{28,32},{32,36}... | collective-permute-start | bytes 1179656 | tf_op jit(solution)/shard_map/ppermute | solution.py:334
  9.4 1.0 copy-start.1
  10.3 4.1 %copy-start = (bf16[1,128,512]{2,1,0:T(8,128)(2,1)S(1)}, bf16[1,128,512]{2,1,0:T(8,128)(2,1)}, u32[]{:S(2)}) copy-start(bf16[1,128,512]{2,1,0:T(8,128)(2,1)} %process_hbm.1) | copy-start | bytes 393220
  15.9 13.8 %all-to-all-start = ((f32[4,320,128]{2,1,0:T(8,128)}), f32[4,320,128]{2,1,0:T(8,128)S(1)}, u32[]{:S(2)}, u32[]{:S(2)}) async-start(f32[4,320,128]{2,1,0:T(8,128)} %get-tuple-element.36), calls=%async_computation | async-start | bytes 1310720 | tf_op jit(solution)/shard_map/all_to_all | solution.py:338
  20.2 9.6 %copy-start.2 = (f32[1,128]{1,0:T(1,128)S(1)}, f32[1,128]{1,0:T(1,128)}, u32[]{:S(2)}) copy-start(f32[1,128]{1,0:T(1,128)} %prior_ref.1) | copy-start | bytes 1540
  42.2 17.7 %all-to-all-start.2 = ((bf16[4,256,512]{2,1,0:T(8,128)(2,1)}), bf16[4,256,512]{2,1,0:T(8,128)(2,1)S(1)}, u32[]{:S(2)}, u32[]{:S(2)}) async-start(bf16[4,256,512]{2,1,0:T(8,128)(2,1)} %get-tuple-element.41), calls=%async_computation.2 | async-start | bytes 2097152 | tf_op jit(solution)/shard_map/all_to_all | solution.py:338
  61.3 11.2 %collective-permute-start.1 = (f32[320,128]{1,0:T(8,128)S(1)}, f32[320,128]{1,0:T(8,128)S(1)}, u32[]{:S(2)}, u32[]{:S(2)}) collective-permute-start(f32[320,128]{1,0:T(8,128)S(1)} %get-tuple-element.44), channel_id=1, source_target_pairs={{4,0},{8,4},{12,8},{16,12},{20,16},{24,20},{28,24},{32,28},{36,32}... | collective-permute-start | bytes 491528 | tf_op jit(solution)/shard_map/ppermute | solution.py:334
  65.5 7.0 %collective-permute-start.2 = (f32[320,128]{1,0:T(8,128)S(1)}, f32[320,128]{1,0:T(8,128)S(1)}, u32[]{:S(2)}, u32[]{:S(2)}) collective-permute-start(f32[320,128]{1,0:T(8,128)S(1)} %get-tuple-element.45), channel_id=1, source_target_pairs={{0,4},{4,8},{8,12},{12,16},{16,20},{20,24},{24,28},{28,32},{32,36}... | collective-permute-start | bytes 491528 | tf_op jit(solution)/shard_map/ppermute | solution.py:334
  73.3 14.4 %all-to-all-start.3 = ((f32[4,320,128]{2,1,0:T(8,128)}), f32[4,320,128]{2,1,0:T(8,128)S(1)}, u32[]{:S(2)}, u32[]{:S(2)}) async-start(f32[4,320,128]{2,1,0:T(8,128)} %get-tuple-element.50), calls=%async_computation.3 | async-start | bytes 1310720 | tf_op jit(solution)/shard_map/all_to_all | solution.py:338
  77.6 23.2 %collective-permute-start.3 = (f32[512,512]{1,0:T(8,128)}, f32[512,512]{1,0:T(8,128)S(1)}, u32[]{:S(2)}, u32[]{:S(2)}) collective-permute-start(f32[512,512]{1,0:T(8,128)} %coupling.2), channel_id=1, source_target_pairs={{0,4},{4,8},{8,12},{12,16},{16,20},{20,24},{24,28},{28,32},{32,36}... | collective-permute-start | bytes 3145736 | tf_op jit(solution)/shard_map/ppermute | solution.py:334
  85.8 19.6 %collective-permute-start.4 = (f32[512,512]{1,0:T(8,128)}, f32[512,512]{1,0:T(8,128)S(1)}, u32[]{:S(2)}, u32[]{:S(2)}) collective-permute-start(f32[512,512]{1,0:T(8,128)} %coupling.2), channel_id=1, source_target_pairs={{4,0},{8,4},{12,8},{16,12},{20,16},{24,20},{28,24},{32,28},{36,32}... | collective-permute-start | bytes 3145736 | tf_op jit(solution)/shard_map/ppermute | solution.py:334
  107.1 15.9 %collective-permute-start.5 = (f32[320,128]{1,0:T(8,128)S(1)}, f32[320,128]{1,0:T(8,128)S(1)}, u32[]{:S(2)}, u32[]{:S(2)}) collective-permute-start(f32[320,128]{1,0:T(8,128)S(1)} %get-tuple-element.53), channel_id=1, source_target_pairs={{8,0},{12,4},{16,8},{20,12},{24,16},{28,20},{32,24},{36,28},{40,32... | collective-permute-start | bytes 491528 | tf_op jit(solution)/shard_map/ppermute | solution.py:334
  109.0 14.0 %collective-permute-start.6 = (f32[320,128]{1,0:T(8,128)S(1)}, f32[320,128]{1,0:T(8,128)S(1)}, u32[]{:S(2)}, u32[]{:S(2)}) collective-permute-start(f32[320,128]{1,0:T(8,128)S(1)} %get-tuple-element.54), channel_id=1, source_target_pairs={{0,8},{4,12},{8,16},{12,20},{16,24},{20,28},{24,32},{28,36},{32,40... | collective-permute-start | bytes 491528 | tf_op jit(solution)/shard_map/ppermute | solution.py:334
  117.7 30.6 %collective-permute-start.7 = (f32[512,512]{1,0:T(8,128)S(1)}, f32[512,512]{1,0:T(8,128)S(1)}, u32[]{:S(2)}, u32[]{:S(2)}) collective-permute-start(f32[512,512]{1,0:T(8,128)S(1)} %coupling.3), channel_id=1, source_target_pairs={{0,8},{4,12},{8,16},{12,20},{16,24},{20,28},{24,32},{28,36},{32,40... | collective-permute-start | bytes 3145736 | tf_op jit(solution)/shard_map/ppermute | solution.py:334
  119.6 28.7 %collective-permute-start.8 = (f32[512,512]{1,0:T(8,128)S(1)}, f32[512,512]{1,0:T(8,128)S(1)}, u32[]{:S(2)}, u32[]{:S(2)}) collective-permute-start(f32[512,512]{1,0:T(8,128)S(1)} %coupling.3), channel_id=1, source_target_pairs={{8,0},{12,4},{16,8},{20,12},{24,16},{28,20},{32,24},{36,28},{40,32... | collective-permute-start | bytes 3145736 | tf_op jit(solution)/shard_map/ppermute | solution.py:334
  149.1 20.7 %collective-permute-start.9 = (f32[128,512]{1,0:T(8,128)S(1)}, f32[128,512]{1,0:T(8,128)S(1)}, u32[]{:S(2)}, u32[]{:S(2)}) collective-permute-start(f32[128,512]{1,0:T(8,128)S(1)} %row_coupling.1), channel_id=1, source_target_pairs={{16,0},{20,4},{24,8},{28,12},{32,16},{36,20},{40,24},{44,28},{48,3... | collective-permute-start | bytes 786440 | tf_op jit(solution)/shard_map/ppermute | solution.py:334
  152.5 21.4 %collective-permute-start.11 = (bf16[128,512]{1,0:T(8,128)(2,1)S(1)}, bf16[128,512]{1,0:T(8,128)(2,1)S(1)}, u32[]{:S(2)}, u32[]{:S(2)}) collective-permute-start(bf16[128,512]{1,0:T(8,128)(2,1)S(1)} %get-tuple-element.64), channel_id=1, source_target_pairs={{16,0},{20,4},{24,8},{28,12},{32,16},{36,20},{40,24},{44,28},{48,3... | collective-permute-start | bytes 393224 | tf_op jit(solution)/shard_map/ppermute | solution.py:334
  154.4 19.5 %collective-permute-start.10 = (bf16[128,512]{1,0:T(8,128)(2,1)S(1)}, bf16[128,512]{1,0:T(8,128)(2,1)S(1)}, u32[]{:S(2)}, u32[]{:S(2)}) collective-permute-start(bf16[128,512]{1,0:T(8,128)(2,1)S(1)} %get-tuple-element.63), channel_id=1, source_target_pairs={{0,16},{4,20},{8,24},{12,28},{16,32},{20,36},{24,40},{28,44},{32,4... | collective-permute-start | bytes 393224 | tf_op jit(solution)/shard_map/ppermute | solution.py:334

commit v4 on v3

--- a/solution.py
+++ b/solution.py
@@ -273,8 +273,8 @@
     col = pl.multiple_of(sid_ref[0] * NB, NB)
     lhs = jnp.concatenate([a_ref[pl.ds(col, NB), :], c_ref[:, pl.ds(col, NB)].T], axis=0)
     z = halves(split_dot(halves(lhs), halves(x_ref[...])))
-    right_term[...] = cross_dot((z[0][:NB], z[1][:NB]), a_ref[...], MK).astype(bf16)
-    left_term[...] = cross_dot((z[0][NB:], z[1][NB:]), c_ref[...]).astype(bf16)
+    right_term[...] = cross_dot((z[0][:NB], z[1][:NB]), a_ref[...], MK)
+    left_term[...] = cross_dot((z[0][NB:], z[1][NB:]), c_ref[...])
 
 
 def row_coupling_kernel(sid_ref, x_ref, a_ref, c_ref, n_ref):
@@ -398,7 +398,7 @@
             (n,) = row_call(row_coupling_kernel, (f32,), sids, x, a, c, "row_coupling")
             coupling = passed_along(n, "tm", -distance)
             x, n = lax.optimization_barrier((x, n))
-            right_term, left_term = row_call(row_terms_kernel, (bf16, bf16), sids, x, a, c, "row_terms")
+            right_term, left_term = row_call(row_terms_kernel, (f32, f32), sids, x, a, c, "row_terms")
             from_right = passed_along(right_term, "tm", -distance)
             from_left = passed_along(left_term, "tm", distance)
             coupling = pl.pallas_call(
@@ -411,7 +411,7 @@
                 name="negate",
             )(coupling)
             rows, coupling = lax.optimization_barrier((rows, coupling))
-            return ((rows - from_left.astype(f32) - from_right.astype(f32))[None], coupling[None])
+            return ((rows - from_left - from_right)[None], coupling[None])
         right_term, left_term = sliced_terms(sids, x, a, c)
         x, right_term, left_term = lax.optimization_barrier((x, right_term, left_term))
         from_right = passed_along(right_term, "tm", -distance)

time: 175 us -> 181 us (1.034)
  the two profiles are of different devices: /device:TPU:251 before, /device:TPU:255 now
where the time goes in v4:
time: 181 us; the launch traced here: 180 us
  starting transfers between devices  63.2 us (35%)
  Pallas kernels  55.7 us (31%)
  waiting for transfers between devices  34.9 us (19%)
  blocking collectives  23.2 us (13%)
    ppermute x12, starting transfers between devices, passed_along(): return lax.ppermute(block, axis, route)  49.5 us
    pallas_call x3, Pallas kernels, inverse(): pl.pallas_call(functools.partial(inverse_kernel, with_rows), out_shape=ou...  39 us
    ppermute x12, waiting for transfers between devices, passed_along(): return lax.ppermute(block, axis, route)  26 us
    all_to_all x2, blocking collectives, exchanged(): return lax.all_to_all(blocks, 'swath', 0, 0, tiled=True)  23.2 us
    all_to_all x3, starting transfers between devices, exchanged(): return lax.all_to_all(blocks, 'swath', 0, 0, tiled=True)  13.7 us
    all_to_all x3, waiting for transfers between devices, exchanged(): return lax.all_to_all(blocks, 'swath', 0, 0, tiled=True)  8.98 us
    pallas_call x2, Pallas kernels, coupled(): pl.pallas_call(coupling_kernel, out_shape=jax.ShapeDtypeStruct(x.shape, f...  4.06 us
  transfers between devices with their start and end apart: 15, of which 6 were waited for; matrix products, arithmetic and copies ran while one was open for 0% of the time, Pallas kernels for 26%

profile of v4, /device:TPU:255, one launch (start us, length us, event | category | flops | bytes accessed | tf_op | source)
XLA Modules:
  0.0 180.4 jit_solution(9119182207123057502)
XLA Ops:
  1.3 3.1 %weigh.1 = (bf16[256,512]{1,0:T(8,128)(2,1)}, bf16[384,512]{1,0:T(8,128)(2,1)}) custom-call(s32[1,1]{1,0:T(1,128)S(6)} %copy.7.counts_ref, s32[1,4]{1,0:T(1,128)} %routes_ref.1, bf16[1,512,512]{2,1,0:T(8,128)(2,1)} %design_hbm.1, bf16[1,128,512]{2,1,0:T(8,128)(2,1)} %process_hbm.1), custom_call_target="tpu_custom_call" | custom-call | tf_op jit(solution)/shard_map/weigh/pallas_call | solution.py:348
  4.4 5.0 %collective-permute-start = (bf16[384,512]{1,0:T(8,128)(2,1)}, bf16[384,512]{1,0:T(8,128)(2,1)S(1)}, u32[]{:S(2)}, u32[]{:S(2)}) collective-permute-start(bf16[384,512]{1,0:T(8,128)(2,1)} %get-tuple-element.35), channel_id=1, source_target_pairs={{0,4},{4,8},{8,12},{12,16},{16,20},{20,24},{24,28},{28,32},{32,36}... | collective-permute-start | bytes 1179656 | tf_op jit(solution)/shard_map/ppermute | solution.py:334
  9.4 0.0 copy-start.1
  9.4 0.9 copy-done.1
  10.3 0.3 own_gram.1.g_ref
  10.6 3.7 %collective-permute-done.incoming_ref = bf16[384,512]{1,0:T(8,128)(2,1)S(1)} collective-permute-done((bf16[384,512]{1,0:T(8,128)(2,1)}, bf16[384,512]{1,0:T(8,128)(2,1)S(1)}, u32[]{:S(2)}, u32[]{:S(2)}) %collective-permute-start) | collective-permute-done | bytes 393248 | tf_op jit(solution)/shard_map/ppermute | solution.py:334
  14.4 1.6 gram.1
  15.9 4.2 %all-to-all-start = ((f32[4,320,128]{2,1,0:T(8,128)}), f32[4,320,128]{2,1,0:T(8,128)S(1)}, u32[]{:S(2)}, u32[]{:S(2)}) async-start(f32[4,320,128]{2,1,0:T(8,128)} %get-tuple-element.36), calls=%async_computation | async-start | bytes 1310720 | tf_op jit(solution)/shard_map/all_to_all | solution.py:338
  20.2 9.0 %all-to-all-done.parts_ref = f32[4,320,128]{2,1,0:T(8,128)S(1)} async-done(((f32[4,320,128]{2,1,0:T(8,128)}), f32[4,320,128]{2,1,0:T(8,128)S(1)}, u32[]{:S(2)}, u32[]{:S(2)}) %all-to-all-start) | async-done | bytes 655392 | tf_op jit(solution)/shard_map/all_to_all | solution.py:338
  29.1 0.1 start.1
  29.3 12.2 %all_to_all.25.g_ref = f32[4,320,128]{2,1,0:T(8,128)S(1)} all-to-all(f32[4,320,128]{2,1,0:T(8,128)S(1)} %get-tuple-element.40), channel_id=1, replica_groups=mesh['tm'=128,'swath'=4] {'swath'}, dimensions={0} | all-to-all | bytes 1310720 | tf_op jit(solution)/shard_map/all_to_all | solution.py:338
  41.5 5.3 %all-to-all-start.2 = ((bf16[4,256,512]{2,1,0:T(8,128)(2,1)}), bf16[4,256,512]{2,1,0:T(8,128)(2,1)S(1)}, u32[]{:S(2)}, u32[]{:S(2)}) async-start(bf16[4,256,512]{2,1,0:T(8,128)(2,1)} %get-tuple-element.41), calls=%async_computation.2 | async-start | bytes 2097152 | tf_op jit(solution)/shard_map/all_to_all | solution.py:338
  46.8 13.0 %inverse.3.x_ref = f32[512,512]{1,0:T(8,128)S(1)} custom-call(s32[1]{0:T(128)} %bitcast.sid_ref, f32[4,320,128]{2,1,0:T(8,128)S(1)} %all_to_all.25.g_ref), custom_call_target="tpu_custom_call" | custom-call | flops 8053063680 | bytes 2097152 | tf_op jit(solution)/shard_map/inverse/pallas_call | solution.py:133
  59.8 0.0 all-to-all-done.2
  59.8 0.1 fusion
  59.9 1.3 sliced_terms.2
  61.2 4.2 %collective-permute-start.1 = (f32[320,128]{1,0:T(8,128)S(1)}, f32[320,128]{1,0:T(8,128)S(1)}, u32[]{:S(2)}, u32[]{:S(2)}) collective-permute-start(f32[320,128]{1,0:T(8,128)S(1)} %get-tuple-element.44), channel_id=1, source_target_pairs={{4,0},{8,4},{12,8},{16,12},{20,16},{24,20},{28,24},{32,28},{36,32}... | collective-permute-start | bytes 491528 | tf_op jit(solution)/shard_map/ppermute | solution.py:334
  65.4 4.7 %collective-permute-start.2 = (f32[320,128]{1,0:T(8,128)S(1)}, f32[320,128]{1,0:T(8,128)S(1)}, u32[]{:S(2)}, u32[]{:S(2)}) collective-permute-start(f32[320,128]{1,0:T(8,128)S(1)} %get-tuple-element.45), channel_id=1, source_target_pairs={{0,4},{4,8},{8,12},{12,16},{16,20},{20,24},{24,28},{28,32},{32,36}... | collective-permute-start | bytes 491528 | tf_op jit(solution)/shard_map/ppermute | solution.py:334
  70.1 2.3 %coupling.2 = f32[512,512]{1,0:T(8,128)} custom-call(f32[512,512]{1,0:T(8,128)S(1)} %inverse.3.x_ref, bf16[512,512]{1,0:T(8,128)(2,1)S(1)} %bitcast.10, bf16[512,512]{1,0:T(8,128)(2,1)S(1)} %bitcast.8), custom_call_target="tpu_custom_call" | custom-call | flops 1610612736 | bytes 4194304 | tf_op jit(solution)/shard_map/coupling/pallas_call | solution.py:320
  72.4 0.0 collective-permute-done.1.right_ref
  72.4 0.0 collective-permute-done.2.left_ref
  72.4 0.9 next.2
  73.3 4.2 %all-to-all-start.3 = ((f32[4,320,128]{2,1,0:T(8,128)}), f32[4,320,128]{2,1,0:T(8,128)S(1)}, u32[]{:S(2)}, u32[]{:S(2)}) async-start(f32[4,320,128]{2,1,0:T(8,128)} %get-tuple-element.50), calls=%async_computation.3 | async-start | bytes 1310720 | tf_op jit(solution)/shard_map/all_to_all | solution.py:338
  77.6 8.2 %collective-permute-start.3 = (f32[512,512]{1,0:T(8,128)}, f32[512,512]{1,0:T(8,128)S(1)}, u32[]{:S(2)}, u32[]{:S(2)}) collective-permute-start(f32[512,512]{1,0:T(8,128)} %coupling.2), channel_id=1, source_target_pairs={{0,4},{4,8},{8,12},{12,16},{16,20},{20,24},{24,28},{28,32},{32,36}... | collective-permute-start | bytes 3145736 | tf_op jit(solution)/shard_map/ppermute | solution.py:334
  85.8 1.9 %collective-permute-start.4 = (f32[512,512]{1,0:T(8,128)}, f32[512,512]{1,0:T(8,128)S(1)}, u32[]{:S(2)}, u32[]{:S(2)}) collective-permute-start(f32[512,512]{1,0:T(8,128)} %coupling.2), channel_id=1, source_target_pairs={{4,0},{8,4},{12,8},{16,12},{20,16},{24,20},{28,24},{32,28},{36,32}... | collective-permute-start | bytes 3145736 | tf_op jit(solution)/shard_map/ppermute | solution.py:334
  87.7 0.0 all-to-all-done.3.g_ref
  87.7 13.0 %inverse.4.x_ref = f32[512,512]{1,0:T(8,128)S(1)} custom-call(s32[1]{0:T(128)} %bitcast.sid_ref, f32[4,320,128]{2,1,0:T(8,128)S(1)} %all-to-all-done.3.g_ref), custom_call_target="tpu_custom_call" | custom-call | flops 8053063680 | bytes 2097152 | tf_op jit(solution)/shard_map/inverse/pallas_call | solution.py:133
  100.8 4.7 %collective-permute-done.4.c_ref = f32[512,512]{1,0:T(8,128)S(1)} collective-permute-done((f32[512,512]{1,0:T(8,128)}, f32[512,512]{1,0:T(8,128)S(1)}, u32[]{:S(2)}, u32[]{:S(2)}) %collective-permute-start.4) | collective-permute-done | bytes 1048608 | tf_op jit(solution)/shard_map/ppermute | solution.py:334
  105.4 1.6 sliced_terms.3
  107.0 1.9 %collective-permute-start.5 = (f32[320,128]{1,0:T(8,128)S(1)}, f32[320,128]{1,0:T(8,128)S(1)}, u32[]{:S(2)}, u32[]{:S(2)}) collective-permute-start(f32[320,128]{1,0:T(8,128)S(1)} %get-tuple-element.53), channel_id=1, source_target_pairs={{8,0},{12,4},{16,8},{20,12},{24,16},{28,20},{32,24},{36,28},{40,32... | collective-permute-start | bytes 491528 | tf_op jit(solution)/shard_map/ppermute | solution.py:334
  108.9 6.9 %collective-permute-start.6 = (f32[320,128]{1,0:T(8,128)S(1)}, f32[320,128]{1,0:T(8,128)S(1)}, u32[]{:S(2)}, u32[]{:S(2)}) collective-permute-start(f32[320,128]{1,0:T(8,128)S(1)} %get-tuple-element.54), channel_id=1, source_target_pairs={{0,8},{4,12},{8,16},{12,20},{16,24},{20,28},{24,32},{28,36},{32,40... | collective-permute-start | bytes 491528 | tf_op jit(solution)/shard_map/ppermute | solution.py:334
  115.8 1.8 coupling.3
  117.6 1.9 %collective-permute-start.7 = (f32[512,512]{1,0:T(8,128)S(1)}, f32[512,512]{1,0:T(8,128)S(1)}, u32[]{:S(2)}, u32[]{:S(2)}) collective-permute-start(f32[512,512]{1,0:T(8,128)S(1)} %coupling.3), channel_id=1, source_target_pairs={{0,8},{4,12},{8,16},{12,20},{16,24},{20,28},{24,32},{28,36},{32,40... | collective-permute-start | bytes 3145736 | tf_op jit(solution)/shard_map/ppermute | solution.py:334
  119.6 3.4 %collective-permute-start.8 = (f32[512,512]{1,0:T(8,128)S(1)}, f32[512,512]{1,0:T(8,128)S(1)}, u32[]{:S(2)}, u32[]{:S(2)}) collective-permute-start(f32[512,512]{1,0:T(8,128)S(1)} %coupling.3), channel_id=1, source_target_pairs={{8,0},{12,4},{16,8},{20,12},{24,16},{28,20},{32,24},{36,28},{40,32... | collective-permute-start | bytes 3145736 | tf_op jit(solution)/shard_map/ppermute | solution.py:334
  122.9 0.0 collective-permute-done.6.left_ref
  122.9 0.7 next.3
  123.7 10.9 %all_to_all.26.g_ref = f32[4,320,128]{2,1,0:T(8,128)S(1)} all-to-all(f32[4,320,128]{2,1,0:T(8,128)S(1)} %get-tuple-element.58), channel_id=1, replica_groups=mesh['tm'=128,'swath'=4] {'swath'}, dimensions={0} | all-to-all | bytes 1310720 | tf_op jit(solution)/shard_map/all_to_all | solution.py:338
  134.6 13.0 %inverse.5 = (f32[512,512]{1,0:T(8,128)S(1)}, f32[128,512]{1,0:T(8,128)S(1)}) custom-call(s32[1]{0:T(128)} %bitcast.sid_ref, f32[4,320,128]{2,1,0:T(8,128)S(1)} %all_to_all.26.g_ref), custom_call_target="tpu_custom_call" | custom-call | flops 5368709120 | bytes 2097152 | tf_op jit(solution)/shard_map/inverse/pallas_call | solution.py:133
  147.7 0.5 collective-permute-done.8.c_ref
  148.1 0.8 row_coupling.1
  148.9 1.9 %collective-permute-start.9 = (f32[128,512]{1,0:T(8,128)S(1)}, f32[128,512]{1,0:T(8,128)S(1)}, u32[]{:S(2)}, u32[]{:S(2)}) collective-permute-start(f32[128,512]{1,0:T(8,128)S(1)} %row_coupling.1), channel_id=1, source_target_pairs={{16,0},{20,4},{24,8},{28,12},{32,16},{36,20},{40,24},{44,28},{48,3... | collective-permute-start | bytes 786440 | tf_op jit(solution)/shard_map/ppermute | solution.py:334
  150.9 1.4 row_terms.1
  152.3 1.9 %collective-permute-start.11 = (f32[128,512]{1,0:T(8,128)S(1)}, f32[128,512]{1,0:T(8,128)S(1)}, u32[]{:S(2)}, u32[]{:S(2)}) collective-permute-start(f32[128,512]{1,0:T(8,128)S(1)} %get-tuple-element.64), channel_id=1, source_target_pairs={{16,0},{20,4},{24,8},{28,12},{32,16},{36,20},{40,24},{44,28},{48,3... | collective-permute-start | bytes 786440 | tf_op jit(solution)/shard_map/ppermute | solution.py:334
  154.3 7.6 %collective-permute-start.10 = (f32[128,512]{1,0:T(8,128)S(1)}, f32[128,512]{1,0:T(8,128)S(1)}, u32[]{:S(2)}, u32[]{:S(2)}) collective-permute-start(f32[128,512]{1,0:T(8,128)S(1)} %get-tuple-element.63), channel_id=1, source_target_pairs={{0,16},{4,20},{8,24},{12,28},{16,32},{20,36},{24,40},{28,44},{32,4... | collective-permute-start | bytes 786440 | tf_op jit(solution)/shard_map/ppermute | solution.py:334
  161.8 10.9 %collective-permute-done.9.n_ref = f32[128,512]{1,0:T(8,128)S(1)} collective-permute-done((f32[128,512]{1,0:T(8,128)S(1)}, f32[128,512]{1,0:T(8,128)S(1)}, u32[]{:S(2)}, u32[]{:S(2)}) %collective-permute-start.9) | collective-permute-done | bytes 262176 | tf_op jit(solution)/shard_map/ppermute | solution.py:334
  172.8 0.7 negate.1
  173.5 6.1 %collective-permute-done.11 = f32[128,512]{1,0:T(8,128)S(1)} collective-permute-done((f32[128,512]{1,0:T(8,128)S(1)}, f32[128,512]{1,0:T(8,128)S(1)}, u32[]{:S(2)}, u32[]{:S(2)}) %collective-permute-start.11) | collective-permute-done | bytes 262176 | tf_op jit(solution)/shard_map/ppermute | solution.py:334
  179.6 0.8 subtract_bitcast_fusion
  (8 shorter events, 0.0 us)
Async XLA Ops:
  4.4 10.0 %collective-permute-start = (bf16[384,512]{1,0:T(8,128)(2,1)}, bf16[384,512]{1,0:T(8,128)(2,1)S(1)}, u32[]{:S(2)}, u32[]{:S(2)}) collective-permute-start(bf16[384,512]{1,0:T(8,128)(2,1)} %get-tuple-element.35), channel_id=1, source_target_pairs={{0,4},{4,8},{8,12},{12,16},{16,20},{20,24},{24,28},{28,32},{32,36}... | collective-permute-start | bytes 1179656 | tf_op jit(solution)/shard_map/ppermute | solution.py:334
  9.4 1.0 copy-start.1
  10.3 4.1 %copy-start = (bf16[1,128,512]{2,1,0:T(8,128)(2,1)S(1)}, bf16[1,128,512]{2,1,0:T(8,128)(2,1)}, u32[]{:S(2)}) copy-start(bf16[1,128,512]{2,1,0:T(8,128)(2,1)} %process_hbm.1) | copy-start | bytes 393220
  15.9 13.2 %all-to-all-start = ((f32[4,320,128]{2,1,0:T(8,128)}), f32[4,320,128]{2,1,0:T(8,128)S(1)}, u32[]{:S(2)}, u32[]{:S(2)}) async-start(f32[4,320,128]{2,1,0:T(8,128)} %get-tuple-element.36), calls=%async_computation | async-start | bytes 1310720 | tf_op jit(solution)/shard_map/all_to_all | solution.py:338
  20.2 9.0 %copy-start.2 = (f32[1,128]{1,0:T(1,128)S(1)}, f32[1,128]{1,0:T(1,128)}, u32[]{:S(2)}) copy-start(f32[1,128]{1,0:T(1,128)} %prior_ref.1) | copy-start | bytes 1540
  41.5 18.3 %all-to-all-start.2 = ((bf16[4,256,512]{2,1,0:T(8,128)(2,1)}), bf16[4,256,512]{2,1,0:T(8,128)(2,1)S(1)}, u32[]{:S(2)}, u32[]{:S(2)}) async-start(bf16[4,256,512]{2,1,0:T(8,128)(2,1)} %get-tuple-element.41), calls=%async_computation.2 | async-start | bytes 2097152 | tf_op jit(solution)/shard_map/all_to_all | solution.py:338
  61.2 11.2 %collective-permute-start.1 = (f32[320,128]{1,0:T(8,128)S(1)}, f32[320,128]{1,0:T(8,128)S(1)}, u32[]{:S(2)}, u32[]{:S(2)}) collective-permute-start(f32[320,128]{1,0:T(8,128)S(1)} %get-tuple-element.44), channel_id=1, source_target_pairs={{4,0},{8,4},{12,8},{16,12},{20,16},{24,20},{28,24},{32,28},{36,32}... | collective-permute-start | bytes 491528 | tf_op jit(solution)/shard_map/ppermute | solution.py:334
  65.4 7.0 %collective-permute-start.2 = (f32[320,128]{1,0:T(8,128)S(1)}, f32[320,128]{1,0:T(8,128)S(1)}, u32[]{:S(2)}, u32[]{:S(2)}) collective-permute-start(f32[320,128]{1,0:T(8,128)S(1)} %get-tuple-element.45), channel_id=1, source_target_pairs={{0,4},{4,8},{8,12},{12,16},{16,20},{20,24},{24,28},{28,32},{32,36}... | collective-permute-start | bytes 491528 | tf_op jit(solution)/shard_map/ppermute | solution.py:334
  73.3 14.4 %all-to-all-start.3 = ((f32[4,320,128]{2,1,0:T(8,128)}), f32[4,320,128]{2,1,0:T(8,128)S(1)}, u32[]{:S(2)}, u32[]{:S(2)}) async-start(f32[4,320,128]{2,1,0:T(8,128)} %get-tuple-element.50), calls=%async_computation.3 | async-start | bytes 1310720 | tf_op jit(solution)/shard_map/all_to_all | solution.py:338
  77.6 23.2 %collective-permute-start.3 = (f32[512,512]{1,0:T(8,128)}, f32[512,512]{1,0:T(8,128)S(1)}, u32[]{:S(2)}, u32[]{:S(2)}) collective-permute-start(f32[512,512]{1,0:T(8,128)} %coupling.2), channel_id=1, source_target_pairs={{0,4},{4,8},{8,12},{12,16},{16,20},{20,24},{24,28},{28,32},{32,36}... | collective-permute-start | bytes 3145736 | tf_op jit(solution)/shard_map/ppermute | solution.py:334
  85.8 19.6 %collective-permute-start.4 = (f32[512,512]{1,0:T(8,128)}, f32[512,512]{1,0:T(8,128)S(1)}, u32[]{:S(2)}, u32[]{:S(2)}) collective-permute-start(f32[512,512]{1,0:T(8,128)} %coupling.2), channel_id=1, source_target_pairs={{4,0},{8,4},{12,8},{16,12},{20,16},{24,20},{28,24},{32,28},{36,32}... | collective-permute-start | bytes 3145736 | tf_op jit(solution)/shard_map/ppermute | solution.py:334
  107.0 15.9 %collective-permute-start.5 = (f32[320,128]{1,0:T(8,128)S(1)}, f32[320,128]{1,0:T(8,128)S(1)}, u32[]{:S(2)}, u32[]{:S(2)}) collective-permute-start(f32[320,128]{1,0:T(8,128)S(1)} %get-tuple-element.53), channel_id=1, source_target_pairs={{8,0},{12,4},{16,8},{20,12},{24,16},{28,20},{32,24},{36,28},{40,32... | collective-permute-start | bytes 491528 | tf_op jit(solution)/shard_map/ppermute | solution.py:334
  108.9 14.0 %collective-permute-start.6 = (f32[320,128]{1,0:T(8,128)S(1)}, f32[320,128]{1,0:T(8,128)S(1)}, u32[]{:S(2)}, u32[]{:S(2)}) collective-permute-start(f32[320,128]{1,0:T(8,128)S(1)} %get-tuple-element.54), channel_id=1, source_target_pairs={{0,8},{4,12},{8,16},{12,20},{16,24},{20,28},{24,32},{28,36},{32,40... | collective-permute-start | bytes 491528 | tf_op jit(solution)/shard_map/ppermute | solution.py:334
  117.6 30.0 %collective-permute-start.7 = (f32[512,512]{1,0:T(8,128)S(1)}, f32[512,512]{1,0:T(8,128)S(1)}, u32[]{:S(2)}, u32[]{:S(2)}) collective-permute-start(f32[512,512]{1,0:T(8,128)S(1)} %coupling.3), channel_id=1, source_target_pairs={{0,8},{4,12},{8,16},{12,20},{16,24},{20,28},{24,32},{28,36},{32,40... | collective-permute-start | bytes 3145736 | tf_op jit(solution)/shard_map/ppermute | solution.py:334
  119.6 28.6 %collective-permute-start.8 = (f32[512,512]{1,0:T(8,128)S(1)}, f32[512,512]{1,0:T(8,128)S(1)}, u32[]{:S(2)}, u32[]{:S(2)}) collective-permute-start(f32[512,512]{1,0:T(8,128)S(1)} %coupling.3), channel_id=1, source_target_pairs={{8,0},{12,4},{16,8},{20,12},{24,16},{28,20},{32,24},{36,28},{40,32... | collective-permute-start | bytes 3145736 | tf_op jit(solution)/shard_map/ppermute | solution.py:334
  148.9 23.8 %collective-permute-start.9 = (f32[128,512]{1,0:T(8,128)S(1)}, f32[128,512]{1,0:T(8,128)S(1)}, u32[]{:S(2)}, u32[]{:S(2)}) collective-permute-start(f32[128,512]{1,0:T(8,128)S(1)} %row_coupling.1), channel_id=1, source_target_pairs={{16,0},{20,4},{24,8},{28,12},{32,16},{36,20},{40,24},{44,28},{48,3... | collective-permute-start | bytes 786440 | tf_op jit(solution)/shard_map/ppermute | solution.py:334
  152.3 27.3 %collective-permute-start.11 = (f32[128,512]{1,0:T(8,128)S(1)}, f32[128,512]{1,0:T(8,128)S(1)}, u32[]{:S(2)}, u32[]{:S(2)}) collective-permute-start(f32[128,512]{1,0:T(8,128)S(1)} %get-tuple-element.64), channel_id=1, source_target_pairs={{16,0},{20,4},{24,8},{28,12},{32,16},{36,20},{40,24},{44,28},{48,3... | collective-permute-start | bytes 786440 | tf_op jit(solution)/shard_map/ppermute | solution.py:334
  154.3 25.4 %collective-permute-start.10 = (f32[128,512]{1,0:T(8,128)S(1)}, f32[128,512]{1,0:T(8,128)S(1)}, u32[]{:S(2)}, u32[]{:S(2)}) collective-permute-start(f32[128,512]{1,0:T(8,128)S(1)} %get-tuple-element.63), channel_id=1, source_target_pairs={{0,16},{4,20},{8,24},{12,28},{16,32},{20,36},{24,40},{28,44},{32,4... | collective-permute-start | bytes 786440 | tf_op jit(solution)/shard_map/ppermute | solution.py:334

commit v5 on v4

--- a/solution.py
+++ b/solution.py
@@ -137,7 +137,7 @@
         out_specs=[VMEM] * len(outs),
         scratch_shapes=[pltpu.VMEM((size, NB), f32)],
         compiler_params=PARAMS,
-        cost_estimate=pl.CostEstimate(flops=40*size**3 if with_rows else 60 * size**3, bytes_accessed=8 * size * size, transcendentals=0),
+        cost_estimate=pl.CostEstimate(flops=40 * size**3, bytes_accessed=8 * size * size, transcendentals=0),
         name="inverse",
     )(sid, g)
 

time: 181 us -> 179 us (0.989)
  the two profiles are of different devices: /device:TPU:255 before, /device:TPU:248 now
where the time goes in v5:
time: 179 us; the launch traced here: 178 us
  Pallas kernels  53.8 us (30%)
  starting transfers between devices  47.2 us (26%)
  blocking collectives  40.9 us (23%)
  waiting for transfers between devices  33.1 us (18%)
    all_to_all x3, blocking collectives, exchanged(): return lax.all_to_all(blocks, 'swath', 0, 0, tiled=True)  40.9 us
    ppermute x12, starting transfers between devices, passed_along(): return lax.ppermute(block, axis, route)  39.4 us
    pallas_call x3, Pallas kernels, inverse(): pl.pallas_call(functools.partial(inverse_kernel, with_rows), out_shape=ou...  39 us
    ppermute x12, waiting for transfers between devices, passed_along(): return lax.ppermute(block, axis, route)  20.5 us
    all_to_all x2, waiting for transfers between devices, exchanged(): return lax.all_to_all(blocks, 'swath', 0, 0, tiled=True)  12.6 us
    all_to_all x2, starting transfers between devices, exchanged(): return lax.all_to_all(blocks, 'swath', 0, 0, tiled=True)  7.81 us
  transfers between devices with their start and end apart: 14, of which 5 were waited for; matrix products, arithmetic and copies ran while one was open for 0% of the time, Pallas kernels for 25%

profile of v5, /device:TPU:248, one launch (start us, length us, event | category | flops | bytes accessed | tf_op | source)
XLA Modules:
  0.0 178.4 jit_solution(2791864313254822724)
XLA Ops:
  1.3 3.1 %weigh.1 = (bf16[256,512]{1,0:T(8,128)(2,1)}, bf16[384,512]{1,0:T(8,128)(2,1)}) custom-call(s32[1,1]{1,0:T(1,128)S(6)} %copy.7.counts_ref, s32[1,4]{1,0:T(1,128)} %routes_ref.1, bf16[1,512,512]{2,1,0:T(8,128)(2,1)} %design_hbm.1, bf16[1,128,512]{2,1,0:T(8,128)(2,1)} %process_hbm.1), custom_call_target="tpu_custom_call" | custom-call | tf_op jit(solution)/shard_map/weigh/pallas_call | solution.py:348
  4.4 1.9 %collective-permute-start = (bf16[384,512]{1,0:T(8,128)(2,1)}, bf16[384,512]{1,0:T(8,128)(2,1)S(1)}, u32[]{:S(2)}, u32[]{:S(2)}) collective-permute-start(bf16[384,512]{1,0:T(8,128)(2,1)} %get-tuple-element.35), channel_id=1, source_target_pairs={{0,4},{4,8},{8,12},{12,16},{16,20},{20,24},{24,28},{28,32},{32,36}... | collective-permute-start | bytes 1179656 | tf_op jit(solution)/shard_map/ppermute | solution.py:334
  6.3 0.0 copy-start.1
  6.3 0.9 copy-done.1
  7.3 0.3 own_gram.1.g_ref
  7.6 6.1 %collective-permute-done.incoming_ref = bf16[384,512]{1,0:T(8,128)(2,1)S(1)} collective-permute-done((bf16[384,512]{1,0:T(8,128)(2,1)}, bf16[384,512]{1,0:T(8,128)(2,1)S(1)}, u32[]{:S(2)}, u32[]{:S(2)}) %collective-permute-start) | collective-permute-done | bytes 393248 | tf_op jit(solution)/shard_map/ppermute | solution.py:334
  13.7 1.5 gram.1
  15.2 4.3 %all-to-all-start = ((f32[4,320,128]{2,1,0:T(8,128)}), f32[4,320,128]{2,1,0:T(8,128)S(1)}, u32[]{:S(2)}, u32[]{:S(2)}) async-start(f32[4,320,128]{2,1,0:T(8,128)} %get-tuple-element.36), calls=%async_computation | async-start | bytes 1310720 | tf_op jit(solution)/shard_map/all_to_all | solution.py:338
  19.5 11.6 %all-to-all-done.parts_ref = f32[4,320,128]{2,1,0:T(8,128)S(1)} async-done(((f32[4,320,128]{2,1,0:T(8,128)}), f32[4,320,128]{2,1,0:T(8,128)S(1)}, u32[]{:S(2)}, u32[]{:S(2)}) %all-to-all-start) | async-done | bytes 655392 | tf_op jit(solution)/shard_map/all_to_all | solution.py:338
  31.1 0.1 start.1
  31.2 13.2 %all_to_all.25.g_ref = f32[4,320,128]{2,1,0:T(8,128)S(1)} all-to-all(f32[4,320,128]{2,1,0:T(8,128)S(1)} %get-tuple-element.40), channel_id=1, replica_groups=mesh['tm'=128,'swath'=4] {'swath'}, dimensions={0} | all-to-all | bytes 1310720 | tf_op jit(solution)/shard_map/all_to_all | solution.py:338
  44.4 3.5 %all-to-all-start.2 = ((bf16[4,256,512]{2,1,0:T(8,128)(2,1)}), bf16[4,256,512]{2,1,0:T(8,128)(2,1)S(1)}, u32[]{:S(2)}, u32[]{:S(2)}) async-start(bf16[4,256,512]{2,1,0:T(8,128)(2,1)} %get-tuple-element.41), calls=%async_computation.2 | async-start | bytes 2097152 | tf_op jit(solution)/shard_map/all_to_all | solution.py:338
  47.9 13.0 %inverse.3.x_ref = f32[512,512]{1,0:T(8,128)S(1)} custom-call(s32[1]{0:T(128)} %bitcast.sid_ref, f32[4,320,128]{2,1,0:T(8,128)S(1)} %all_to_all.25.g_ref), custom_call_target="tpu_custom_call" | custom-call | flops 5368709120 | bytes 2097152 | tf_op jit(solution)/shard_map/inverse/pallas_call | solution.py:133
  60.9 1.0 all-to-all-done.2
  61.9 0.1 fusion
  62.1 1.3 sliced_terms.2
  63.3 1.9 %collective-permute-start.1 = (f32[320,128]{1,0:T(8,128)S(1)}, f32[320,128]{1,0:T(8,128)S(1)}, u32[]{:S(2)}, u32[]{:S(2)}) collective-permute-start(f32[320,128]{1,0:T(8,128)S(1)} %get-tuple-element.44), channel_id=1, source_target_pairs={{4,0},{8,4},{12,8},{16,12},{20,16},{24,20},{28,24},{32,28},{36,32}... | collective-permute-start | bytes 491528 | tf_op jit(solution)/shard_map/ppermute | solution.py:334
  65.3 2.4 %collective-permute-start.2 = (f32[320,128]{1,0:T(8,128)S(1)}, f32[320,128]{1,0:T(8,128)S(1)}, u32[]{:S(2)}, u32[]{:S(2)}) collective-permute-start(f32[320,128]{1,0:T(8,128)S(1)} %get-tuple-element.45), channel_id=1, source_target_pairs={{0,4},{4,8},{8,12},{12,16},{16,20},{20,24},{24,28},{28,32},{32,36}... | collective-permute-start | bytes 491528 | tf_op jit(solution)/shard_map/ppermute | solution.py:334
  67.7 1.3 coupling.2
  69.0 4.1 %collective-permute-start.3 = (f32[512,512]{1,0:T(8,128)S(1)}, f32[512,512]{1,0:T(8,128)S(1)}, u32[]{:S(2)}, u32[]{:S(2)}) collective-permute-start(f32[512,512]{1,0:T(8,128)S(1)} %coupling.2), channel_id=1, source_target_pairs={{0,4},{4,8},{8,12},{12,16},{16,20},{20,24},{24,28},{28,32},{32,36}... | collective-permute-start | bytes 3145736 | tf_op jit(solution)/shard_map/ppermute | solution.py:334
  73.1 1.9 %collective-permute-start.4 = (f32[512,512]{1,0:T(8,128)S(1)}, f32[512,512]{1,0:T(8,128)S(1)}, u32[]{:S(2)}, u32[]{:S(2)}) collective-permute-start(f32[512,512]{1,0:T(8,128)S(1)} %coupling.2), channel_id=1, source_target_pairs={{4,0},{8,4},{12,8},{16,12},{20,16},{24,20},{28,24},{32,28},{36,32}... | collective-permute-start | bytes 3145736 | tf_op jit(solution)/shard_map/ppermute | solution.py:334
  75.0 0.0 collective-permute-done.2.left_ref
  75.0 0.1 next.2
  75.1 15.8 %all_to_all.26.g_ref = f32[4,320,128]{2,1,0:T(8,128)S(1)} all-to-all(f32[4,320,128]{2,1,0:T(8,128)S(1)} %get-tuple-element.50), channel_id=1, replica_groups=mesh['tm'=128,'swath'=4] {'swath'}, dimensions={0} | all-to-all | bytes 1310720 | tf_op jit(solution)/shard_map/all_to_all | solution.py:338
  90.8 13.0 %inverse.4.x_ref = f32[512,512]{1,0:T(8,128)S(1)} custom-call(s32[1]{0:T(128)} %bitcast.sid_ref, f32[4,320,128]{2,1,0:T(8,128)S(1)} %all_to_all.26.g_ref), custom_call_target="tpu_custom_call" | custom-call | flops 5368709120 | bytes 2097152 | tf_op jit(solution)/shard_map/inverse/pallas_call | solution.py:133
  103.8 0.0 collective-permute-done.3.a_ref
  103.9 0.0 collective-permute-done.4.c_ref
  103.9 1.5 sliced_terms.3
  105.4 1.9 %collective-permute-start.5 = (f32[320,128]{1,0:T(8,128)S(1)}, f32[320,128]{1,0:T(8,128)S(1)}, u32[]{:S(2)}, u32[]{:S(2)}) collective-permute-start(f32[320,128]{1,0:T(8,128)S(1)} %get-tuple-element.53), channel_id=1, source_target_pairs={{8,0},{12,4},{16,8},{20,12},{24,16},{28,20},{32,24},{36,28},{40,32... | collective-permute-start | bytes 491528 | tf_op jit(solution)/shard_map/ppermute | solution.py:334
  107.3 7.4 %collective-permute-start.6 = (f32[320,128]{1,0:T(8,128)S(1)}, f32[320,128]{1,0:T(8,128)S(1)}, u32[]{:S(2)}, u32[]{:S(2)}) collective-permute-start(f32[320,128]{1,0:T(8,128)S(1)} %get-tuple-element.54), channel_id=1, source_target_pairs={{0,8},{4,12},{8,16},{12,20},{16,24},{20,28},{24,32},{28,36},{32,40... | collective-permute-start | bytes 491528 | tf_op jit(solution)/shard_map/ppermute | solution.py:334
  114.8 1.8 %coupling.3 = f32[512,512]{1,0:T(8,128)S(1)} custom-call(f32[512,512]{1,0:T(8,128)S(1)} %inverse.4.x_ref, f32[512,512]{1,0:T(8,128)S(1)} %collective-permute-done.3.a_ref, f32[512,512]{1,0:T(8,128)S(1)} %collective-permute-done.4.c_ref), custom_call_target="tpu_custom_call" | custom-call | flops 1610612736 | bytes 4194304 | tf_op jit(solution)/shard_map/coupling/pallas_call | solution.py:320
  116.6 1.9 %collective-permute-start.7 = (f32[512,512]{1,0:T(8,128)S(1)}, f32[512,512]{1,0:T(8,128)S(1)}, u32[]{:S(2)}, u32[]{:S(2)}) collective-permute-start(f32[512,512]{1,0:T(8,128)S(1)} %coupling.3), channel_id=1, source_target_pairs={{0,8},{4,12},{8,16},{12,20},{16,24},{20,28},{24,32},{28,36},{32,40... | collective-permute-start | bytes 3145736 | tf_op jit(solution)/shard_map/ppermute | solution.py:334
  118.5 3.9 %collective-permute-start.8 = (f32[512,512]{1,0:T(8,128)S(1)}, f32[512,512]{1,0:T(8,128)S(1)}, u32[]{:S(2)}, u32[]{:S(2)}) collective-permute-start(f32[512,512]{1,0:T(8,128)S(1)} %coupling.3), channel_id=1, source_target_pairs={{8,0},{12,4},{16,8},{20,12},{24,16},{28,20},{32,24},{36,28},{40,32... | collective-permute-start | bytes 3145736 | tf_op jit(solution)/shard_map/ppermute | solution.py:334
  122.5 0.7 next.3
  123.2 12.0 %all_to_all.27.g_ref = f32[4,320,128]{2,1,0:T(8,128)S(1)} all-to-all(f32[4,320,128]{2,1,0:T(8,128)S(1)} %get-tuple-element.58), channel_id=1, replica_groups=mesh['tm'=128,'swath'=4] {'swath'}, dimensions={0} | all-to-all | bytes 1310720 | tf_op jit(solution)/shard_map/all_to_all | solution.py:338
  135.2 13.0 %inverse.5 = (f32[512,512]{1,0:T(8,128)S(1)}, f32[128,512]{1,0:T(8,128)S(1)}) custom-call(s32[1]{0:T(128)} %bitcast.sid_ref, f32[4,320,128]{2,1,0:T(8,128)S(1)} %all_to_all.27.g_ref), custom_call_target="tpu_custom_call" | custom-call | flops 5368709120 | bytes 2097152 | tf_op jit(solution)/shard_map/inverse/pallas_call | solution.py:133
  148.2 0.0 collective-permute-done.7.a_ref
  148.2 0.0 collective-permute-done.8.c_ref
  148.2 0.8 row_coupling.1
  149.0 1.9 %collective-permute-start.9 = (f32[128,512]{1,0:T(8,128)S(1)}, f32[128,512]{1,0:T(8,128)S(1)}, u32[]{:S(2)}, u32[]{:S(2)}) collective-permute-start(f32[128,512]{1,0:T(8,128)S(1)} %row_coupling.1), channel_id=1, source_target_pairs={{16,0},{20,4},{24,8},{28,12},{32,16},{36,20},{40,24},{44,28},{48,3... | collective-permute-start | bytes 786440 | tf_op jit(solution)/shard_map/ppermute | solution.py:334
  151.0 1.4 row_terms.1
  152.4 1.9 %collective-permute-start.11 = (f32[128,512]{1,0:T(8,128)S(1)}, f32[128,512]{1,0:T(8,128)S(1)}, u32[]{:S(2)}, u32[]{:S(2)}) collective-permute-start(f32[128,512]{1,0:T(8,128)S(1)} %get-tuple-element.64), channel_id=1, source_target_pairs={{16,0},{20,4},{24,8},{28,12},{32,16},{36,20},{40,24},{44,28},{48,3... | collective-permute-start | bytes 786440 | tf_op jit(solution)/shard_map/ppermute | solution.py:334
  154.3 8.1 %collective-permute-start.10 = (f32[128,512]{1,0:T(8,128)S(1)}, f32[128,512]{1,0:T(8,128)S(1)}, u32[]{:S(2)}, u32[]{:S(2)}) collective-permute-start(f32[128,512]{1,0:T(8,128)S(1)} %get-tuple-element.63), channel_id=1, source_target_pairs={{0,16},{4,20},{8,24},{12,28},{16,32},{20,36},{24,40},{28,44},{32,4... | collective-permute-start | bytes 786440 | tf_op jit(solution)/shard_map/ppermute | solution.py:334
  162.5 10.8 %collective-permute-done.9.n_ref = f32[128,512]{1,0:T(8,128)S(1)} collective-permute-done((f32[128,512]{1,0:T(8,128)S(1)}, f32[128,512]{1,0:T(8,128)S(1)}, u32[]{:S(2)}, u32[]{:S(2)}) %collective-permute-start.9) | collective-permute-done | bytes 262176 | tf_op jit(solution)/shard_map/ppermute | solution.py:334
  173.2 0.7 negate.1
  174.0 3.7 %collective-permute-done.11 = f32[128,512]{1,0:T(8,128)S(1)} collective-permute-done((f32[128,512]{1,0:T(8,128)S(1)}, f32[128,512]{1,0:T(8,128)S(1)}, u32[]{:S(2)}, u32[]{:S(2)}) %collective-permute-start.11) | collective-permute-done | bytes 262176 | tf_op jit(solution)/shard_map/ppermute | solution.py:334
  177.6 0.0 collective-permute-done.10
  177.6 0.8 subtract_bitcast_fusion
  (7 shorter events, 0.0 us)
Async XLA Ops:
  4.4 9.3 %collective-permute-start = (bf16[384,512]{1,0:T(8,128)(2,1)}, bf16[384,512]{1,0:T(8,128)(2,1)S(1)}, u32[]{:S(2)}, u32[]{:S(2)}) collective-permute-start(bf16[384,512]{1,0:T(8,128)(2,1)} %get-tuple-element.35), channel_id=1, source_target_pairs={{0,4},{4,8},{8,12},{12,16},{16,20},{20,24},{24,28},{28,32},{32,36}... | collective-permute-start | bytes 1179656 | tf_op jit(solution)/shard_map/ppermute | solution.py:334
  6.3 1.0 copy-start.1
  7.3 6.4 %copy-start = (bf16[1,128,512]{2,1,0:T(8,128)(2,1)S(1)}, bf16[1,128,512]{2,1,0:T(8,128)(2,1)}, u32[]{:S(2)}) copy-start(bf16[1,128,512]{2,1,0:T(8,128)(2,1)} %process_hbm.1) | copy-start | bytes 393220
  15.2 15.9 %all-to-all-start = ((f32[4,320,128]{2,1,0:T(8,128)}), f32[4,320,128]{2,1,0:T(8,128)S(1)}, u32[]{:S(2)}, u32[]{:S(2)}) async-start(f32[4,320,128]{2,1,0:T(8,128)} %get-tuple-element.36), calls=%async_computation | async-start | bytes 1310720 | tf_op jit(solution)/shard_map/all_to_all | solution.py:338
  19.5 11.6 %copy-start.2 = (f32[1,128]{1,0:T(1,128)S(1)}, f32[1,128]{1,0:T(1,128)}, u32[]{:S(2)}) copy-start(f32[1,128]{1,0:T(1,128)} %prior_ref.1) | copy-start | bytes 1540
  44.4 17.5 %all-to-all-start.2 = ((bf16[4,256,512]{2,1,0:T(8,128)(2,1)}), bf16[4,256,512]{2,1,0:T(8,128)(2,1)S(1)}, u32[]{:S(2)}, u32[]{:S(2)}) async-start(bf16[4,256,512]{2,1,0:T(8,128)(2,1)} %get-tuple-element.41), calls=%async_computation.2 | async-start | bytes 2097152 | tf_op jit(solution)/shard_map/all_to_all | solution.py:338
  63.3 11.6 %collective-permute-start.1 = (f32[320,128]{1,0:T(8,128)S(1)}, f32[320,128]{1,0:T(8,128)S(1)}, u32[]{:S(2)}, u32[]{:S(2)}) collective-permute-start(f32[320,128]{1,0:T(8,128)S(1)} %get-tuple-element.44), channel_id=1, source_target_pairs={{4,0},{8,4},{12,8},{16,12},{20,16},{24,20},{28,24},{32,28},{36,32}... | collective-permute-start | bytes 491528 | tf_op jit(solution)/shard_map/ppermute | solution.py:334
  65.3 9.7 %collective-permute-start.2 = (f32[320,128]{1,0:T(8,128)S(1)}, f32[320,128]{1,0:T(8,128)S(1)}, u32[]{:S(2)}, u32[]{:S(2)}) collective-permute-start(f32[320,128]{1,0:T(8,128)S(1)} %get-tuple-element.45), channel_id=1, source_target_pairs={{0,4},{4,8},{8,12},{12,16},{16,20},{20,24},{24,28},{28,32},{32,36}... | collective-permute-start | bytes 491528 | tf_op jit(solution)/shard_map/ppermute | solution.py:334
  69.0 34.9 %collective-permute-start.3 = (f32[512,512]{1,0:T(8,128)S(1)}, f32[512,512]{1,0:T(8,128)S(1)}, u32[]{:S(2)}, u32[]{:S(2)}) collective-permute-start(f32[512,512]{1,0:T(8,128)S(1)} %coupling.2), channel_id=1, source_target_pairs={{0,4},{4,8},{8,12},{12,16},{16,20},{20,24},{24,28},{28,32},{32,36}... | collective-permute-start | bytes 3145736 | tf_op jit(solution)/shard_map/ppermute | solution.py:334
  73.1 30.8 %collective-permute-start.4 = (f32[512,512]{1,0:T(8,128)S(1)}, f32[512,512]{1,0:T(8,128)S(1)}, u32[]{:S(2)}, u32[]{:S(2)}) collective-permute-start(f32[512,512]{1,0:T(8,128)S(1)} %coupling.2), channel_id=1, source_target_pairs={{4,0},{8,4},{12,8},{16,12},{20,16},{24,20},{28,24},{32,28},{36,32}... | collective-permute-start | bytes 3145736 | tf_op jit(solution)/shard_map/ppermute | solution.py:334
  105.4 17.0 %collective-permute-start.5 = (f32[320,128]{1,0:T(8,128)S(1)}, f32[320,128]{1,0:T(8,128)S(1)}, u32[]{:S(2)}, u32[]{:S(2)}) collective-permute-start(f32[320,128]{1,0:T(8,128)S(1)} %get-tuple-element.53), channel_id=1, source_target_pairs={{8,0},{12,4},{16,8},{20,12},{24,16},{28,20},{32,24},{36,28},{40,32... | collective-permute-start | bytes 491528 | tf_op jit(solution)/shard_map/ppermute | solution.py:334
  107.3 15.1 %collective-permute-start.6 = (f32[320,128]{1,0:T(8,128)S(1)}, f32[320,128]{1,0:T(8,128)S(1)}, u32[]{:S(2)}, u32[]{:S(2)}) collective-permute-start(f32[320,128]{1,0:T(8,128)S(1)} %get-tuple-element.54), channel_id=1, source_target_pairs={{0,8},{4,12},{8,16},{12,20},{16,24},{20,28},{24,32},{28,36},{32,40... | collective-permute-start | bytes 491528 | tf_op jit(solution)/shard_map/ppermute | solution.py:334
  116.6 31.6 %collective-permute-start.7 = (f32[512,512]{1,0:T(8,128)S(1)}, f32[512,512]{1,0:T(8,128)S(1)}, u32[]{:S(2)}, u32[]{:S(2)}) collective-permute-start(f32[512,512]{1,0:T(8,128)S(1)} %coupling.3), channel_id=1, source_target_pairs={{0,8},{4,12},{8,16},{12,20},{16,24},{20,28},{24,32},{28,36},{32,40... | collective-permute-start | bytes 3145736 | tf_op jit(solution)/shard_map/ppermute | solution.py:334
  118.5 29.7 %collective-permute-start.8 = (f32[512,512]{1,0:T(8,128)S(1)}, f32[512,512]{1,0:T(8,128)S(1)}, u32[]{:S(2)}, u32[]{:S(2)}) collective-permute-start(f32[512,512]{1,0:T(8,128)S(1)} %coupling.3), channel_id=1, source_target_pairs={{8,0},{12,4},{16,8},{20,12},{24,16},{28,20},{32,24},{36,28},{40,32... | collective-permute-start | bytes 3145736 | tf_op jit(solution)/shard_map/ppermute | solution.py:334
  149.0 24.2 %collective-permute-start.9 = (f32[128,512]{1,0:T(8,128)S(1)}, f32[128,512]{1,0:T(8,128)S(1)}, u32[]{:S(2)}, u32[]{:S(2)}) collective-permute-start(f32[128,512]{1,0:T(8,128)S(1)} %row_coupling.1), channel_id=1, source_target_pairs={{16,0},{20,4},{24,8},{28,12},{32,16},{36,20},{40,24},{44,28},{48,3... | collective-permute-start | bytes 786440 | tf_op jit(solution)/shard_map/ppermute | solution.py:334
  152.4 25.2 %collective-permute-start.11 = (f32[128,512]{1,0:T(8,128)S(1)}, f32[128,512]{1,0:T(8,128)S(1)}, u32[]{:S(2)}, u32[]{:S(2)}) collective-permute-start(f32[128,512]{1,0:T(8,128)S(1)} %get-tuple-element.64), channel_id=1, source_target_pairs={{16,0},{20,4},{24,8},{28,12},{32,16},{36,20},{40,24},{44,28},{48,3... | collective-permute-start | bytes 786440 | tf_op jit(solution)/shard_map/ppermute | solution.py:334
  154.3 23.3 %collective-permute-start.10 = (f32[128,512]{1,0:T(8,128)S(1)}, f32[128,512]{1,0:T(8,128)S(1)}, u32[]{:S(2)}, u32[]{:S(2)}) collective-permute-start(f32[128,512]{1,0:T(8,128)S(1)} %get-tuple-element.63), channel_id=1, source_target_pairs={{0,16},{4,20},{8,24},{12,28},{16,32},{20,36},{24,40},{28,44},{32,4... | collective-permute-start | bytes 786440 | tf_op jit(solution)/shard_map/ppermute | solution.py:334
